TPU v7x, 512 devices: a whole 4x8x8 slice. The times are simulated.
512 devices in a mesh: grp: 2 (over x_lo), seq: 32 (over x_hi, z, core), tile: 8 (over y).
Axes of the slice: x: 4 (x_hi: 2, x_lo: 2; x = x_hi * 2 + x_lo), y: 8, z: 8, core: 2. Of those that a mesh axis runs over, the one named last changes fastest.
Arguments:
- enc_features: bfloat16 [8, 80, 64, 512], P('tile', None, 'seq'), may hold values from -6 to 6
- conv_weight: bfloat16 [3, 3, 3, 512, 16], replicated, may hold values from -0.0546875 to 0.0546875
- conv_bias: float32 [16], replicated, may hold values from -0.1 to 0.1
- embed_weight: bfloat16 [64, 4096], replicated, may hold values from -0.75 to 0.75
- embed_bias: float32 [4096], replicated, may hold values from -0.1 to 0.1
- mod_shift: float32 [4096], replicated, may hold values from -0.1 to 0.1
- mod_scale: float32 [4096], replicated, may hold values from -2 to 2
- qkv_weight: bfloat16 [4096, 3, 16, 128], P(None, None, ('grp', 'tile')), may hold values from -0.09375 to 0.09375
- q_gain: float32 [128], replicated, may hold values from 1.5 to 2.5
- k_gain: float32 [128], replicated, may hold values from 1.5 to 2.5
Outputs:
- attended: bfloat16 [32, 16, 20, 2048], P('seq', ('grp', 'tile'))
All inputs are finite; a program needn't handle non-finite values.
Results may differ from a plain program's by a relative error of at most 0.015.
Values may be sent and summed in bfloat16 or wider, within the bound.
A program may use at most 64 MiB of HBM per device.

v0:
```python
import math

import jax
import jax.numpy as jnp
from jax import lax
from jax.sharding import PartitionSpec as P


def padded(cells, sides, width):
    for axis, dim in sides:
        count = lax.axis_size(axis)
        ends = count - 1
        head = lax.slice_in_dim(cells, 0, width, axis=dim)
        tail = lax.slice_in_dim(cells, cells.shape[dim] - width, cells.shape[dim], axis=dim)
        cells = jnp.concatenate(
            [
                lax.ppermute(tail, axis, [(i, (i + 1) % count) for i in range(ends)]),
                cells,
                lax.ppermute(head, axis, [((i + 1) % count, i) for i in range(ends)]),
            ],
            axis=dim,
        )
    return cells


def head_norm(raw, gain):
    scale = lax.rsqrt(jnp.mean(raw * raw, axis=-1, keepdims=True) + 1e-06)
    return (raw * scale * gain).astype(jnp.bfloat16)


def local(
    enc_features,
    conv_weight,
    conv_bias,
    embed_weight,
    embed_bias,
    mod_shift,
    mod_scale,
    qkv_weight,
    q_gain,
    k_gain,
):
    frames, rows, cols, chans = enc_features.shape
    zch = conv_weight.shape[4]
    rimmed = padded(enc_features, (("seq", 2), ("tile", 0)), 1)
    rimmed = jnp.pad(rimmed, ((0, 0), (1, 1), (0, 0), (0, 0)))
    windows = []
    for a_tap in range(3):
        for b_tap in range(3):
            for e_tap in range(3):
                windows.append(
                    rimmed[a_tap : a_tap + frames, b_tap : b_tap + rows, e_tap : e_tap + cols, :]
                )
    stacked = jnp.concatenate(windows, axis=-1).reshape(frames * rows * cols, 27 * chans)
    summed = jnp.dot(
        stacked, conv_weight.reshape(27 * chans, zch), preferred_element_type=jnp.float32
    )
    latent = (
        (summed + conv_bias).astype(jnp.bfloat16).reshape(frames, rows // 2, 2, cols // 2, 2, zch)
    )
    patches = latent.transpose(0, 1, 3, 2, 4, 5).reshape(frames * (rows // 2), cols // 2, 4 * zch)
    all_frames = lax.all_gather(patches, "tile", axis=0, tiled=True)
    relaid = lax.all_to_all(all_frames, "seq", split_axis=0, concat_axis=1, tiled=True)
    tok_rows = relaid.shape[0] * relaid.shape[1]
    relaid = relaid.reshape(tok_rows, 4 * zch)
    embedded = jnp.dot(relaid, embed_weight, preferred_element_type=jnp.float32) + embed_bias
    inv = lax.rsqrt(jnp.mean(embedded * embedded, axis=-1, keepdims=True) + 1e-06)
    normed = (embedded * inv * (1.0 + mod_scale) + mod_shift).astype(jnp.bfloat16)
    width = qkv_weight.shape[0]
    local_heads = qkv_weight.shape[2]
    head_size = qkv_weight.shape[3]
    projected = jnp.dot(normed, qkv_weight.reshape(width, -1), preferred_element_type=jnp.float32)
    projected = projected.reshape(tok_rows, 3, local_heads, head_size)
    queries = head_norm(projected[:, 0], q_gain)
    keys = head_norm(projected[:, 1], k_gain)
    values = projected[:, 2].astype(jnp.bfloat16)
    factor = 1.0 / math.sqrt(head_size)
    key_piece = lax.all_gather(keys, "seq", axis=0, tiled=True)
    value_piece = lax.all_gather(values, "seq", axis=0, tiled=True)
    scores = (
        jnp.einsum("qhe,khe->hqk", queries, key_piece, preferred_element_type=jnp.float32) * factor
    )
    weights = jnp.exp(scores)
    total = jnp.sum(weights, axis=2)
    numer = jnp.einsum(
        "hqk,khe->qhe",
        weights.astype(jnp.bfloat16),
        value_piece,
        preferred_element_type=jnp.float32,
    )
    numer, total = (numer, total)
    total = total.T
    outputs = (numer / total[:, :, None]).astype(jnp.bfloat16)
    blocks = lax.all_to_all(outputs, ("grp", "tile"), split_axis=0, concat_axis=1, tiled=True)
    return blocks.reshape(1, 1, blocks.shape[0], blocks.shape[1] * blocks.shape[2])


def solution(mesh):
    in_specs = (
        P("tile", None, "seq", None),
        P(),
        P(),
        P(),
        P(),
        P(),
        P(),
        P(None, None, ("grp", "tile"), None),
        P(),
        P(),
    )
    out_specs = P("seq", ("grp", "tile"), None, None)
    return jax.shard_map(local, mesh=mesh, in_specs=in_specs, out_specs=out_specs, check_vma=False)
```

profile of v0, /device:TPU:1, one launch (start us, length us, event | category | flops | bytes accessed | tf_op | source)
XLA Modules:
  0.0 328.9 jit_solution(2108395418982190374)
XLA Ops:
  6.5 1.3 fusion.50
  7.9 5.4 %collective-permute-start = (bf16[1,80,1,512]{3,2,1,0:T(2,128)(2,1)S(1)}, bf16[1,80,1,512]{3,2,1,0:T(2,128)(2,1)S(1)}, u32[]{:S(2)}, u32[]{:S(2)}) collective-permute-start(bf16[1,80,1,512]{3,2,1,0:T(2,128)(2,1)S(1)} %get-tuple-element.5), channel_id=1, source_target_pairs={{0,8},{8,16},{16,24},{24,32},{32,40},{40,48},{48,56},{56,64},{64,7... | collective-permute-start | bytes 245768 | tf_op jit(solution)/shard_map/ppermute | solution.py:17
  13.3 4.8 %collective-permute-start.1 = (bf16[1,80,1,512]{3,2,1,0:T(2,128)(2,1)S(1)}, bf16[1,80,1,512]{3,2,1,0:T(2,128)(2,1)S(1)}, u32[]{:S(2)}, u32[]{:S(2)}) collective-permute-start(bf16[1,80,1,512]{3,2,1,0:T(2,128)(2,1)S(1)} %get-tuple-element.6), channel_id=1, source_target_pairs={{8,0},{16,8},{24,16},{32,24},{40,32},{48,40},{56,48},{64,56},{72,6... | collective-permute-start | bytes 245768 | tf_op jit(solution)/shard_map/ppermute | solution.py:19
  18.1 1.9 collective-permute-done.1
  20.1 1.5 pad_maximum_fusion
  21.5 3.2 collective-permute-start.2
  24.8 1.3 collective-permute-start.3
  26.1 1.4 copy.21
  28.1 1.9 collective-permute-done.2
  30.0 4.1 %collective-permute-done.3 = bf16[1,80,4,512]{3,2,1,0:T(4,128)(2,1)S(1)} collective-permute-done((bf16[1,80,4,512]{3,2,1,0:T(4,128)(2,1)S(1)}, bf16[1,80,4,512]{3,2,1,0:T(4,128)(2,1)S(1)}, u32[]{:S(2)}, u32[]{:S(2)}) %collective-permute-start.3) | collective-permute-done | bytes 327712 | tf_op jit(solution)/shard_map/ppermute | solution.py:19
  34.1 1.8 select_maximum_fusion
  47.9 1.1 fusion.44
  59.2 9.6 %reshape.199 = bf16[160,13824]{1,0:T(8,128)(2,1)} reshape(bf16[1,80,2,13824]{3,2,1,0:T(2,128)(2,1)} %slice_dynamic-update-slice_fusion) | data formatting | bytes 8847360 | tf_op jit(solution)/shard_map/reshape | solution.py:54
  68.7 3.5 %fusion.38 = bf16[160,16]{0,1:T(8,128)(2,1)S(1)} fusion(bf16[160,13824]{1,0:T(8,128)(2,1)} %reshape.199, bf16[13824,16]{0,1:T(8,128)(2,1)S(1)} %reshape.200, f32[16]{0:T(128)S(1)} %copy-done.5), kind=kOutput, calls=%fused_computation.24 | convolution fusion | flops 70784000 | bytes 4871232 | tf_op jit(solution)/shard_map/dot_general | solution.py:55
  72.5 19.4 %all_gather.9 = bf16[320,1,64]{2,0,1:T(8,128)(2,1)S(1)} all-gather(bf16[40,1,64]{2,0,1:T(8,128)(2,1)S(1)} %reshape_transpose_reshape.3), channel_id=1, replica_groups=mesh['grp'=2,'seq'=32,'tile'=8] {'tile'}, dimensions={0}, use_global_device_ids=true | all-gather | bytes 46080 | tf_op jit(solution)/shard_map/all_gather | solution.py:62
  93.8 20.9 %all-to-all-start = ((bf16[32,2,320]{2,1,0:T(2,128)(2,1)}), bf16[32,2,320]{2,1,0:T(2,128)(2,1)S(1)}, u32[]{:S(2)}, u32[]{:S(2)}) async-start(bf16[32,2,320]{2,1,0:T(2,128)(2,1)} %reshape.212), calls=%async_computation | async-start | bytes 98304 | tf_op jit(solution)/shard_map/all_to_all | solution.py:63
  114.9 4.7 %copy.25 = bf16[4096,3,1,128]{0,3,1,2:T(8,128)(2,1)} copy(bf16[4096,3,1,128]{3,0,2,1:T(8,128)(2,1)} %param.17) | data formatting | bytes 6291456 | tf_op args[7]
  119.6 4.4 %all-to-all-done = bf16[32,2,320]{2,1,0:T(2,128)(2,1)S(1)} async-done(((bf16[32,2,320]{2,1,0:T(2,128)(2,1)}), bf16[32,2,320]{2,1,0:T(2,128)(2,1)S(1)}, u32[]{:S(2)}, u32[]{:S(2)}) %all-to-all-start) | async-done | bytes 40992 | tf_op jit(solution)/shard_map/all_to_all | solution.py:63
  126.7 1.6 fusion.13
  130.1 83.2 %all-gather.4.cloned.1.call-done = bf16[10240,1,128]{2,0,1:T(8,128)(2,1)} async-done(((bf16[320,1,128]{2,0,1:T(8,128)(2,1)}), bf16[10240,1,128]{2,0,1:T(8,128)(2,1)}) %all-gather.4.cloned.1.call-update) | async-done | bytes 2621456 | tf_op jit(solution)/shard_map/all_gather | solution.py:78
  213.3 7.1 %fusion.51 = (f32[320]{0:T(512)S(1)}, bf16[320,10240]{1,0:T(8,128)(2,1)}) fusion(bf16[10240,1,128]{2,0,1:T(8,128)(2,1)} %all-gather.4.cloned.1.call-done, f32[320,3,1,128]{3,0,1,2:T(8,128)S(1)} %fusion.13, f32[128]{0:T(128)S(1)} %copy-done.8, f32[320]{0:T(512)S(1)} %add_rsqrt_fusion.1), kind=kOutput, calls=%fused_computation.76 | convolution fusion | flops 848813760 | bytes 9342720 | tf_op jit(solution)/shard_map/qhe,khe->hqk/dot_general | solution.py:81
  220.4 80.5 %all-gather.6.cloned.1.call-done = bf16[10240,1,1,128]{3,0,1,2:T(8,128)(2,1)} async-done(((bf16[320,1,1,128]{3,0,1,2:T(8,128)(2,1)}), bf16[10240,1,1,128]{3,0,1,2:T(8,128)(2,1)}) %all-gather.6.cloned.1.call-update) | async-done | bytes 2621456 | tf_op jit(solution)/shard_map/all_gather | solution.py:79
  300.9 5.5 %fusion.33 = bf16[320,1,128]{2,0,1:T(8,128)(2,1)S(1)} fusion(bf16[10240,1,1,128]{3,0,1,2:T(8,128)(2,1)} %all-gather.6.cloned.1.call-done, bf16[320,10240]{1,0:T(8,128)(2,1)} %get-tuple-element.10, f32[320]{0:T(512)S(1)} %get-tuple-element.9), kind=kOutput, calls=%fused_computation.22 | convolution fusion | flops 838942720 | bytes 9258240 | tf_op jit(solution)/shard_map/hqk,khe->qhe/dot_general | solution.py:85
  307.0 13.8 %all_to_all.30 = bf16[16,2,1280]{2,1,0:T(2,128)(2,1)S(1)} all-to-all(bf16[16,2,1280]{2,1,0:T(2,128)(2,1)S(1)} %reshape.214), channel_id=1, replica_groups=mesh['grp'=2,'seq'=32,'tile'=8] {'grp','tile'}, dimensions={0} | all-to-all | bytes 163840 | tf_op jit(solution)/shard_map/all_to_all | solution.py:94
  (75 shorter events, 31.5 us)
Async XLA Ops:
  6.5 118.2 %copy-start = (bf16[64,4096]{1,0:T(8,128)(2,1)S(1)}, bf16[64,4096]{1,0:T(8,128)(2,1)}, u32[]{:S(2)}) copy-start(bf16[64,4096]{1,0:T(8,128)(2,1)} %param.13) | copy-start | bytes 1572868
  7.9 10.2 %collective-permute-start = (bf16[1,80,1,512]{3,2,1,0:T(2,128)(2,1)S(1)}, bf16[1,80,1,512]{3,2,1,0:T(2,128)(2,1)S(1)}, u32[]{:S(2)}, u32[]{:S(2)}) collective-permute-start(bf16[1,80,1,512]{3,2,1,0:T(2,128)(2,1)S(1)} %get-tuple-element.5), channel_id=1, source_target_pairs={{0,8},{8,16},{16,24},{24,32},{32,40},{40,48},{48,56},{56,64},{64,7... | collective-permute-start | bytes 245768 | tf_op jit(solution)/shard_map/ppermute | solution.py:17
  13.3 32.8 %copy-start.1 = (bf16[1,80,2,512]{3,2,1,0:T(2,128)(2,1)S(1)}, bf16[1,80,2,512]{3,2,1,0:T(2,128)(2,1)}, u32[]{:S(2)}) copy-start(bf16[1,80,2,512]{3,2,1,0:T(2,128)(2,1)} %param.10) | copy-start | bytes 491524
  13.3 6.8 %collective-permute-start.1 = (bf16[1,80,1,512]{3,2,1,0:T(2,128)(2,1)S(1)}, bf16[1,80,1,512]{3,2,1,0:T(2,128)(2,1)S(1)}, u32[]{:S(2)}, u32[]{:S(2)}) collective-permute-start(bf16[1,80,1,512]{3,2,1,0:T(2,128)(2,1)S(1)} %get-tuple-element.6), channel_id=1, source_target_pairs={{8,0},{16,8},{24,16},{32,24},{40,32},{48,40},{56,48},{64,56},{72,6... | collective-permute-start | bytes 245768 | tf_op jit(solution)/shard_map/ppermute | solution.py:19
  21.5 8.4 %collective-permute-start.2 = (bf16[1,80,4,512]{3,2,1,0:T(4,128)(2,1)S(1)}, bf16[1,80,4,512]{3,2,1,0:T(4,128)(2,1)S(1)}, u32[]{:S(2)}, u32[]{:S(2)}) collective-permute-start(bf16[1,80,4,512]{3,2,1,0:T(4,128)(2,1)S(1)} %pad_maximum_fusion), channel_id=1, source_target_pairs={{0,1},{1,2},{2,3},{3,4},{4,5},{5,6},{6,7},{8,9},{9,10},{10,11},{11... | collective-permute-start | bytes 983048 | tf_op jit(solution)/shard_map/ppermute | solution.py:17
  24.8 9.3 %collective-permute-start.3 = (bf16[1,80,4,512]{3,2,1,0:T(4,128)(2,1)S(1)}, bf16[1,80,4,512]{3,2,1,0:T(4,128)(2,1)S(1)}, u32[]{:S(2)}, u32[]{:S(2)}) collective-permute-start(bf16[1,80,4,512]{3,2,1,0:T(4,128)(2,1)S(1)} %pad_maximum_fusion), channel_id=1, source_target_pairs={{1,0},{2,1},{3,2},{4,3},{5,4},{6,5},{7,6},{9,8},{10,9},{11,10},{12... | collective-permute-start | bytes 983048 | tf_op jit(solution)/shard_map/ppermute | solution.py:19
  59.2 9.6 %copy-start.5 = (f32[16]{0:T(128)S(1)}, f32[16]{0:T(128)}, u32[]{:S(2)}) copy-start(f32[16]{0:T(128)} %param.12) | copy-start | bytes 196
  68.7 46.1 %copy-start.4 = (f32[4096]{0:T(1024)S(1)}, f32[4096]{0:T(1024)}, u32[]{:S(2)}) copy-start(f32[4096]{0:T(1024)} %param.16) | copy-start | bytes 49156
  72.2 52.6 %copy-start.3 = (f32[4096]{0:T(1024)S(1)}, f32[4096]{0:T(1024)}, u32[]{:S(2)}) copy-start(f32[4096]{0:T(1024)} %param.14) | copy-start | bytes 49156
  93.8 30.3 %all-to-all-start = ((bf16[32,2,320]{2,1,0:T(2,128)(2,1)}), bf16[32,2,320]{2,1,0:T(2,128)(2,1)S(1)}, u32[]{:S(2)}, u32[]{:S(2)}) async-start(bf16[32,2,320]{2,1,0:T(2,128)(2,1)} %reshape.212), calls=%async_computation | async-start | bytes 98304 | tf_op jit(solution)/shard_map/all_to_all | solution.py:63
  114.6 98.7 %all-gather.4.cloned.1.call-start = ((), (), s32[]{:S(2)}) async-start(), calls=%async_computation.2 | async-start | bytes 2703360 | tf_op jit(solution)/shard_map/all_gather | solution.py:78
  124.8 1.9 copy-start.2
  124.8 1.9 copy-start.7
  126.7 1.7 copy-start.6
  126.7 86.6 %copy-start.8 = (f32[128]{0:T(128)S(1)}, f32[128]{0:T(128)}, u32[]{:S(2)}) copy-start(f32[128]{0:T(128)} %param.18) | copy-start | bytes 1540
  129.2 171.7 %all-gather.6.cloned.1.call-start = ((), (), s32[]{:S(2)}) async-start(), calls=%async_computation.3 | async-start | bytes 2703360 | tf_op jit(solution)/shard_map/all_gather | solution.py:79
Sparse Core Ops, SparseCore 0:
  129.3 83.9 all-gather.3
  216.7 84.1 all-gather.5
where the time goes:
time: 330 us; the launch traced here: 329 us
  waiting for transfers between devices  176 us (53%)
  local copies, waits for them, and re-layouts  42.9 us (13%)
  starting transfers between devices  35.8 us (11%)
  blocking collectives  33.1 us (10%)
  matrix products  18.5 us (6%)
  between operations  13.7 us (4%)
  other arithmetic  8.74 us (3%)
    all_gather x1, waiting for transfers between devices, local(): key_piece = lax.all_gather(keys, 'seq', axis=0, tiled=True)  83.2 us
    all_gather x1, waiting for transfers between devices, local(): value_piece = lax.all_gather(values, 'seq', axis=0, tiled=True)  80.5 us
    unnamed x48, local copies, waits for them, and re-layouts  28.3 us
    all_to_all x1, starting transfers between devices, local(): lax.all_to_all(all_frames, 'seq', split_axis=0, concat_axis=1, tiled=True)  20.9 us
    all_gather x1, blocking collectives, local(): all_frames = lax.all_gather(patches, 'tile', axis=0, tiled=True)  19.4 us
    all_to_all x1, blocking collectives, local(): lax.all_to_all(outputs, ('grp', 'tile'), split_axis=0, concat_axis=1, til...  13.8 us
    reshape x1, local copies, waits for them, and re-layouts, local(): jnp.concatenate(windows, axis=-1).reshape(frames * rows * cols, 27 * chans)  9.56 us
    ppermute x2, starting transfers between devices, padded(): lax.ppermute(tail, axis, [(i, (i + 1) % count) for i in range(ends)])  8.61 us
  transfers between devices with their start and end apart: 7, of which 6 were waited for; matrix products, arithmetic and copies ran while one was open for 4% of the time, Pallas kernels for 0%

commit v1 on v0

v1 whole, which is shorter than its diff:
```python
import math

import jax
import jax.numpy as jnp
from jax import lax
from jax.experimental import pallas as pl
from jax.experimental.pallas import tpu as pltpu
from jax.sharding import PartitionSpec as P

bf16 = jnp.bfloat16
f32 = jnp.float32

D = 4096
NT = (((1,), (1,)), ((), ()))
EPS = 1e-6


def nt_dot(a, b):
    return lax.dot_general(a, b, NT, preferred_element_type=f32)


def hi_lo(v):
    hi = v.astype(bf16)
    return hi, (v - hi.astype(f32)).astype(bf16)


def conv_block(cw_ref, rho, col):
    zero = jnp.zeros((16, 512), bf16)
    pieces = []
    for a in range(3):
        for ext in range(2):
            for p in range(2):
                for q in range(2):
                    b = rho - p
                    rel = q if ext == 0 else (2 if q == 0 else -1)
                    e = col - rel + 1
                    if 0 <= b <= 2 and 0 <= e <= 2:
                        r = ((a * 3 + b) * 3 + e) * 16
                        pieces.append(cw_ref[r : r + 16, :])
                    else:
                        pieces.append(zero)
    return jnp.concatenate(pieces, axis=0)


def conv_partials(x_ref, cw_ref, g):
    v = x_ref[...].astype(f32).reshape(40, 4, 512)
    part = [v[:, j, :] for j in range(4)]
    edge = jnp.zeros((1, 512), f32)
    acc = None
    for rho in range(4):
        for col in range(2):
            if rho == 0:
                rows = jnp.concatenate([edge, part[2 + col][:39]], axis=0)
            elif rho == 3:
                rows = jnp.concatenate([part[col][1:], edge], axis=0)
            else:
                rows = part[(rho - 1) * 2 + col]
            rows = jnp.where(g == 0, rows[0:24], rows[16:40]).astype(bf16)
            term = nt_dot(rows, conv_block(cw_ref, rho, col))
            acc = term if acc is None else acc + term
    return acc


def kernel(
    x_ref, cw_ref, cbias_ref, emb_hbm, ebias_ref, shift_ref, scale_ref, w_hbm, qg_ref, kg_ref,
    o_ref,
    emb_ref, w_ref, halo_out, halo_in, ybuf, ysend, dens, gat, res, rr, wkv, bias_k, bias_v, gcol,
    kt, vt, qscr, qrows, acc, tot, asend, arecv,
    local_sem, hs_sem, hr_sem, ys_sem, yr_sem, zs_sem, zr_sem, xs_sem, xr_sem, cs_sem, cr_sem, as_sem, ar_sem,
):
    g = lax.axis_index("grp")
    s = lax.axis_index("seq")
    f = lax.axis_index("tile")
    xh, z, core = s // 16, (s // 2) % 8, s % 2
    x = xh * 2 + g
    head = g * 8 + f

    def dev(gg, ss, ff):
        return (gg, ss, ff)

    def x_dev(xx):
        return (xx % 2, (xx // 2) * 16 + z * 2 + core, f)

    def z_dev(zz):
        return (g, xh * 16 + zz * 2 + core, f)

    left, right = lax.rem(s + 31, 32), lax.rem(s + 1, 32)
    before, after = lax.rem(f + 7, 8), lax.rem(f + 1, 8)
    xm, xp, xo = lax.rem(x + 3, 4), lax.rem(x + 1, 4), lax.rem(x + 2, 4)
    partner = (g, s + 1 - 2 * core, f)
    halo_seq = (left, s, right)
    halo_frame = (after, f, before)

    w_copy = pltpu.make_async_copy(w_hbm, w_ref, local_sem.at[0])
    e_copy = pltpu.make_async_copy(emb_hbm, emb_ref, local_sem.at[1])
    e_copy.start()
    w_copy.start()

    barrier = pltpu.get_barrier_semaphore()

    def greet(device):
        pl.semaphore_signal(barrier, inc=1, device_id=device, device_id_type=pl.DeviceIdType.MESH)

    for ss in (left, right):
        for ff in halo_frame:
            greet((g, ss, ff))

    def greet_z(i, _):
        greet(z_dev(lax.rem(z + i, 8)))
        return 0

    lax.fori_loop(1, 8, greet_z, 0)

    def greet_head(i, _):
        j = lax.rem(head + i, 16)
        greet((j // 8, s, j % 8))
        return 0

    lax.fori_loop(1, 16, greet_head, 0)
    greet(x_dev(jnp.where(g == 0, xm, xp)))

    sums = conv_partials(x_ref, cw_ref, g)
    for a in range(3):
        halo_out[a] = sums[:, a * 128 : (a + 1) * 128]
    halo_in[1, 1] = sums[:, 128:256]

    pl.semaphore_wait(barrier, 29)

    def halo_copy(a, t):
        n = a * 3 + t
        return pltpu.make_async_remote_copy(
            src_ref=halo_out.at[a],
            dst_ref=halo_in.at[a, 2 - t],
            send_sem=hs_sem.at[n],
            recv_sem=hr_sem.at[a * 3 + 2 - t],
            device_id=(g, halo_seq[t], halo_frame[a]),
            device_id_type=pl.DeviceIdType.MESH,
        )

    halo = [(a, t) for a in range(3) for t in range(3) if (a, t) != (1, 1)]
    for a, t in halo:
        halo_copy(a, t).start()

    e_copy.wait()
    w_copy.wait()
    res[...] = jnp.zeros_like(res)
    rr[...] = jnp.zeros_like(rr)
    step = 512

    def fold(k, _):
        cols = pl.ds(pl.multiple_of(k * step, step), step)
        e = emb_ref[:, cols]
        gain = 1.0 + scale_ref[:, cols]
        eb = ebias_ref[:, cols]
        e_hi, e_lo = hi_lo(e.astype(f32) * gain)
        rest = jnp.concatenate([eb * gain, shift_ref[:, cols], jnp.zeros((6, step), f32)], axis=0)
        rest_hi, rest_lo = hi_lo(rest)
        rest2 = jnp.concatenate([rest_hi.astype(f32), rest_lo.astype(f32)], axis=0).astype(bf16)
        lhs = jnp.concatenate([e_hi, e_lo, rest2], axis=0)
        w = jnp.concatenate([w_ref[j, cols, :] for j in range(3)], axis=1)
        res[...] += jnp.dot(lhs, w, preferred_element_type=f32)
        b_hi = eb.astype(bf16).astype(f32)
        bias = jnp.concatenate([b_hi, eb - b_hi, jnp.zeros((14, step), f32)], axis=0).astype(bf16)
        both = jnp.concatenate([e, bias, jnp.zeros((48, step), bf16)], axis=0)
        rr[...] += nt_dot(both, both)
        return 0

    lax.fori_loop(0, D // step, fold, 0)

    lane = lax.broadcasted_iota(jnp.int32, (128, 128), 1)
    row = lax.broadcasted_iota(jnp.int32, (128, 128), 0)
    low = lane < 64
    zero64 = jnp.zeros((64, 128), f32)
    for j in range(3):
        cols = slice(j * 128, (j + 1) * 128)
        top = res[0:64, cols] + res[64:128, cols]
        rest = res[128:136, cols] + res[136:144, cols]
        m = jnp.concatenate([top, rest, jnp.zeros((56, 128), f32)], axis=0)
        mt = m.T
        a_t = jnp.where(low, mt, 0.0)
        a_s = pltpu.roll(a_t, 64, 1)
        for half, v in ((0, a_t), (1, a_s)):
            hi, lo = hi_lo(v)
            n = (j * 2 + half) * 128
            wkv[n : n + 128, 0:128] = hi
            wkv[n : n + 128, 128:256] = lo
        if j > 0:
            bias_v_ref = bias_k if j == 1 else bias_v
            bias_v_ref[0] = jnp.broadcast_to(mt[:, 64:65], (128, 128))
            bias_v_ref[1] = jnp.broadcast_to(mt[:, 65:66], (128, 128))
    gram = rr[...]
    g_t = jnp.where(low & (row < 64), gram, 0.0)
    gblock = g_t + pltpu.roll(pltpu.roll(g_t, 64, 1), 64, 0)
    hi, lo = hi_lo(gblock)
    wkv[768:896, 0:128] = hi
    wkv[768:896, 128:256] = lo
    wkv[896:1024, 0:128] = jnp.where(lane == row, 1.0, 0.0).astype(bf16)
    wkv[896:1024, 128:256] = jnp.zeros((128, 128), bf16)
    grow = gram[64:65, :] + gram[65:66, :]
    lane1 = lax.broadcasted_iota(jnp.int32, (1, 128), 1)
    bb = jnp.sum(jnp.where((lane1 == 64) | (lane1 == 65), grow, 0.0), axis=1, keepdims=True)
    grow64 = jnp.where(lane1 < 64, grow, 0.0)
    grow2 = 2.0 * (grow64 + pltpu.roll(grow64, 64, 1))
    gc = gram[:, 64:65] + gram[:, 65:66]
    gc2 = 2.0 * jnp.broadcast_to(jnp.concatenate([gc[0:64], gc[0:64]], axis=0), (128, 128))
    gcol[...] = gc2

    for a, t in halo:
        halo_copy(a, t).wait_recv()
    lane24 = lax.broadcasted_iota(jnp.int32, (24, 128), 1)
    zero24 = jnp.zeros((24, 128), f32)
    has = (f > 0, None, f < 7)
    side = []
    for t in range(3):
        total = None
        for a in range(3):
            v = halo_in[a, t]
            if has[a] is not None:
                v = jnp.where(has[a], v, zero24)
            total = v if total is None else total + v
        side.append(total)
    from_left = jnp.where(s > 0, side[0], zero24)
    from_right = jnp.where(s < 31, side[2], zero24)
    ext = jnp.where((lane24 // 16) % 2 == 0, from_left, from_right)
    lat = side[1] + pltpu.roll(ext, 64, 1)
    cb = jnp.concatenate([cbias_ref[...]] * 8, axis=1)
    lat = (lat + cb).astype(bf16).astype(f32)
    mine = jnp.where(g == 0, lat[0:20], lat[4:24])
    first = mine[0:10]
    second = pltpu.roll(mine[10:20], 64, 1)
    packed = jnp.where(lax.broadcasted_iota(jnp.int32, (10, 128), 1) < 64, first, second)
    packed = jnp.concatenate([packed, jnp.zeros((6, 128), f32)], axis=0).astype(bf16)
    ysend[...] = packed
    ybuf[f] = packed

    def y_copy(i):
        ff = lax.rem(f + i, 8)
        return pltpu.make_async_remote_copy(
            src_ref=ysend, dst_ref=ybuf.at[f], send_sem=ys_sem.at[i], recv_sem=yr_sem.at[i],
            device_id=(g, s, ff), device_id_type=pl.DeviceIdType.MESH,
        )

    for i in range(1, 8):
        y_copy(i).start()

    def y_arrived(i):
        ff = lax.rem(f + 8 - i, 8)
        return pltpu.make_async_remote_copy(
            src_ref=ysend, dst_ref=ybuf.at[ff], send_sem=ys_sem.at[i], recv_sem=yr_sem.at[i],
            device_id=(g, s, ff), device_id_type=pl.DeviceIdType.MESH,
        )

    for i in range(1, 8):
        y_arrived(i).wait_recv()
    for n in range(8):
        dens[n * 10 : n * 10 + 10, :] = ybuf[n, 0:10, :].astype(f32)
    gat[x, core, z] = dens[...].astype(bf16)

    def z_copy(i, zz):
        return pltpu.make_async_remote_copy(
            src_ref=gat.at[x, core, z], dst_ref=gat.at[x, core, z], send_sem=zs_sem.at[i], recv_sem=zr_sem.at[i],
            device_id=z_dev(zz), device_id_type=pl.DeviceIdType.MESH,
        )

    def z_arrived(i, zz):
        return pltpu.make_async_remote_copy(
            src_ref=gat.at[x, core, z], dst_ref=gat.at[x, core, zz], send_sem=zs_sem.at[i], recv_sem=zr_sem.at[i],
            device_id=z_dev(zz), device_id_type=pl.DeviceIdType.MESH,
        )

    for i in (1, 7, 2, 6, 3, 5, 4):
        z_copy(i, lax.rem(z + i, 8)).start()
    for i in (1, 7, 2, 6, 3, 5, 4):
        z_arrived(i, lax.rem(z + 8 - i, 8)).wait_recv()

    def chunk(xx, cc, part):
        ref = gat.at[xx, cc]
        if part == 0:
            return ref
        return ref.at[pl.ds((part - 1) * 4, 4)]

    def x_copy(n, xx, part, to):
        return pltpu.make_async_remote_copy(
            src_ref=chunk(xx, core, part), dst_ref=chunk(xx, core, part), send_sem=xs_sem.at[n],
            recv_sem=xr_sem.at[n], device_id=x_dev(to), device_id_type=pl.DeviceIdType.MESH,
        )

    def c_copy(n, xx, part, cc):
        return pltpu.make_async_remote_copy(
            src_ref=chunk(xx, cc, part), dst_ref=chunk(xx, cc, part), send_sem=cs_sem.at[n],
            recv_sem=cr_sem.at[n], device_id=partner, device_id_type=pl.DeviceIdType.MESH,
        )

    def keys(xx, cc):
        rows = gat[xx, cc].reshape(640, 128)
        p2 = jnp.concatenate([rows, rows], axis=1)
        out = nt_dot(wkv[256:1024, :], p2)
        y = (out[512:640] + jnp.concatenate([gcol[...]] * 5, axis=1)) * out[640:768]
        base = pl.multiple_of((xx * 2 + cc) * 1280, 1280)
        for half in range(2):
            ms = jnp.sum(y[half * 64 : half * 64 + 64], axis=0, keepdims=True) + bb
            inv = lax.rsqrt(jnp.maximum(ms, 0.0) * (1.0 / D) + EPS)
            kr = out[half * 128 : half * 128 + 128]
            kr = (kr + jnp.concatenate([bias_k[0]] * 5, axis=1)) * inv + jnp.concatenate([bias_k[1]] * 5, axis=1)
            ks = lax.rsqrt(jnp.sum(kr * kr, axis=0, keepdims=True) * (1.0 / 128) + EPS)
            cols = pl.ds(base + half * 640, 640)
            kt[:, cols] = (kr * ks).astype(bf16)
            vr = out[256 + half * 128 : 256 + half * 128 + 128]
            vr = (vr + jnp.concatenate([bias_v[0]] * 5, axis=1)) * inv + jnp.concatenate([bias_v[1]] * 5, axis=1)
            vt[:, cols] = vr.astype(bf16)

    other = 1 - core
    x_copy(0, x, 0, xp).start()
    x_copy(1, x, 0, xm).start()
    c_copy(0, x, 0, core).start()
    keys(x, core)
    c_copy(0, x, 0, other).wait_recv()
    keys(x, other)
    x_copy(0, xm, 0, xp).wait_recv()
    x_copy(2, xm, 1, xp).start()
    c_copy(1, xm, 0, core).start()
    x_copy(1, xp, 0, xm).wait_recv()
    x_copy(3, xp, 2, xm).start()
    c_copy(2, xp, 0, core).start()
    keys(xm, core)
    keys(xp, core)
    c_copy(1, xm, 0, other).wait_recv()
    keys(xm, other)
    c_copy(2, xp, 0, other).wait_recv()
    keys(xp, other)
    x_copy(2, xo, 1, xp).wait_recv()
    c_copy(3, xo, 1, core).start()
    x_copy(3, xo, 2, xm).wait_recv()
    c_copy(4, xo, 2, core).start()
    keys(xo, core)
    c_copy(3, xo, 1, other).wait_recv()
    c_copy(4, xo, 2, other).wait_recv()
    keys(xo, other)

    fq, gq, hq = s // 4, (s // 2) % 2, s % 2
    pick_row = lax.broadcasted_iota(jnp.int32, (16, 80), 0)
    pick_col = lax.broadcasted_iota(jnp.int32, (16, 80), 1)
    pick = jnp.where((pick_row < 10) & (pick_col == pick_row + fq * 10), 1.0, 0.0).astype(bf16)
    for hx in range(2):
        blocks = [gat[hx * 2 + gq, cc, zz] for zz in range(8) for cc in range(2)]
        picked = jnp.dot(pick, jnp.concatenate(blocks, axis=1), preferred_element_type=f32)
        for n in range(16):
            qscr[hx * 16 + n] = picked[:, n * 128 : (n + 1) * 128]
    qall = qscr[...]
    for i in range(10):
        qrows[i * 32 : (i + 1) * 32, :] = qall[:, i, :]
    qp = qrows[...]
    qb = qp.astype(bf16)
    q2 = jnp.concatenate([qb, qb], axis=1)
    wq = jnp.where(hq == 0, wkv[0:128, :].astype(f32), wkv[128:256, :].astype(f32)).astype(bf16)
    raw = nt_dot(q2, wq)
    gp = nt_dot(q2, wkv[768:896, :])
    lane320 = lax.broadcasted_iota(jnp.int32, (320, 128), 1)
    y = jnp.where(lane320 // 64 == hq, (gp + grow2) * qp, 0.0)
    ms = jnp.sum(y, axis=1, keepdims=True) + bb
    inv = lax.rsqrt(jnp.maximum(ms, 0.0) * (1.0 / D) + EPS)
    c_q = res[128:129, 0:128] + res[136:137, 0:128]
    d_q = res[129:130, 0:128] + res[137:138, 0:128]
    qr = (raw + c_q) * inv + d_q
    qs = lax.rsqrt(jnp.sum(qr * qr, axis=1, keepdims=True) * (1.0 / 128) + EPS)
    q = (qr * qs * (qg_ref[...] * kg_ref[...] * (math.log2(math.e) / math.sqrt(128.0)))).astype(bf16)

    acc[...] = jnp.zeros_like(acc)
    tot[...] = jnp.zeros_like(tot)
    width = 2560

    def attend(n, _):
        cols = pl.ds(pl.multiple_of(n * width, width), width)
        w = jnp.exp2(jnp.dot(q, kt[:, cols], preferred_element_type=f32))
        t = w[:, 0:128]
        for m in range(1, width // 128):
            t = t + w[:, m * 128 : (m + 1) * 128]
        tot[...] += t
        acc[...] += nt_dot(w.astype(bf16), vt[:, cols])
        return 0

    lax.fori_loop(0, 10240 // width, attend, 0)
    out = acc[...] / jnp.sum(tot[...], axis=1, keepdims=True)
    pad = jnp.zeros((12, 128), f32)
    for j in range(16):
        asend[j] = jnp.concatenate([out[j * 20 : j * 20 + 20], pad], axis=0).astype(bf16)

    def a_copy(i, src, slot, j):
        return pltpu.make_async_remote_copy(
            src_ref=asend.at[src], dst_ref=arecv.at[slot], send_sem=as_sem.at[i], recv_sem=ar_sem.at[i],
            device_id=(j // 8, s, j % 8), device_id_type=pl.DeviceIdType.MESH,
        )

    def send_head(i, _):
        j = lax.rem(head + i, 16)
        a_copy(i, j, head, j).start()
        return 0

    lax.fori_loop(1, 16, send_head, 0)
    arecv[head] = asend[head]

    for a, t in halo:
        halo_copy(a, t).wait_send()
    for i in range(1, 8):
        y_copy(i).wait_send()
        z_copy(i, lax.rem(z + i, 8)).wait_send()
    x_copy(0, x, 0, xp).wait_send()
    x_copy(1, x, 0, xm).wait_send()
    x_copy(2, xm, 1, xp).wait_send()
    x_copy(3, xp, 2, xm).wait_send()
    c_copy(0, x, 0, core).wait_send()
    c_copy(1, xm, 0, core).wait_send()
    c_copy(2, xp, 0, core).wait_send()
    c_copy(3, xo, 1, core).wait_send()
    c_copy(4, xo, 2, core).wait_send()

    def head_arrived(i, _):
        j = lax.rem(head + 16 - i, 16)
        a_copy(i, j, j, j).wait_recv()
        return 0

    lax.fori_loop(1, 16, head_arrived, 0)
    for j in range(16):
        o_ref[:, j * 128 : (j + 1) * 128] = arecv[j, 0:20, :]

    def head_sent(i, _):
        j = lax.rem(head + i, 16)
        a_copy(i, j, head, j).wait_send()
        return 0

    lax.fori_loop(1, 16, head_sent, 0)


def local(
    enc_features, conv_weight, conv_bias, embed_weight, embed_bias, mod_shift, mod_scale, qkv_weight, q_gain, k_gain
):
    vmem = pl.BlockSpec(memory_space=pltpu.VMEM)
    hbm = pl.BlockSpec(memory_space=pl.ANY)
    dma = pltpu.SemaphoreType.DMA
    out = pl.pallas_call(
        kernel,
        out_shape=jax.ShapeDtypeStruct((20, 2048), bf16),
        in_specs=[vmem, vmem, vmem, hbm, vmem, vmem, vmem, hbm, vmem, vmem],
        out_specs=vmem,
        scratch_shapes=[
            pltpu.VMEM((64, D), bf16),
            pltpu.VMEM((3, D, 128), bf16),
            pltpu.VMEM((3, 24, 128), f32),
            pltpu.VMEM((3, 3, 24, 128), f32),
            pltpu.VMEM((8, 16, 128), bf16),
            pltpu.VMEM((16, 128), bf16),
            pltpu.VMEM((80, 128), f32),
            pltpu.VMEM((4, 2, 8, 80, 128), bf16),
            pltpu.VMEM((144, 384), f32),
            pltpu.VMEM((128, 128), f32),
            pltpu.VMEM((1024, 256), bf16),
            pltpu.VMEM((2, 128, 128), f32),
            pltpu.VMEM((2, 128, 128), f32),
            pltpu.VMEM((128, 128), f32),
            pltpu.VMEM((128, 10240), bf16),
            pltpu.VMEM((128, 10240), bf16),
            pltpu.VMEM((32, 16, 128), f32),
            pltpu.VMEM((320, 128), f32),
            pltpu.VMEM((320, 128), f32),
            pltpu.VMEM((320, 128), f32),
            pltpu.VMEM((16, 32, 128), bf16),
            pltpu.VMEM((16, 32, 128), bf16),
            dma((2,)),
            dma((9,)),
            dma((9,)),
            dma((8,)),
            dma((8,)),
            dma((8,)),
            dma((8,)),
            dma((4,)),
            dma((4,)),
            dma((5,)),
            dma((5,)),
            dma((16,)),
            dma((16,)),
        ],
        compiler_params=pltpu.CompilerParams(
            collective_id=0, has_side_effects=True, vmem_limit_bytes=48 * 1024 * 1024
        ),
        cost_estimate=pl.CostEstimate(flops=5_000_000_000, bytes_accessed=6_000_000, transcendentals=3_300_000),
    )(
        enc_features.reshape(80, 2, 512),
        conv_weight.transpose(0, 1, 2, 4, 3).reshape(432, 512),
        conv_bias.reshape(1, 16),
        embed_weight,
        embed_bias.reshape(1, D),
        mod_shift.reshape(1, D),
        mod_scale.reshape(1, D),
        qkv_weight.transpose(1, 2, 0, 3).reshape(3, D, 128),
        q_gain.reshape(1, 128),
        k_gain.reshape(1, 128),
    )
    return out.reshape(1, 1, 20, 2048)


def solution(mesh):
    in_specs = (
        P("tile", None, "seq", None), P(), P(), P(), P(), P(), P(), P(None, None, ("grp", "tile"), None), P(), P(),
    )
    out_specs = P("seq", ("grp", "tile"), None, None)
    return jax.shard_map(local, mesh=mesh, in_specs=in_specs, out_specs=out_specs, check_vma=False)
```

time: 330 us -> 63 us (0.19)
  waiting for transfers between devices: 176 us -> 0 us
  Pallas kernels: 0 us -> 52.4 us
  starting transfers between devices: 35.8 us -> 0 us
  local copies, waits for them, and re-layouts: 42.9 us -> 9.62 us
  blocking collectives: 33.1 us -> 0 us
  matrix products: 18.5 us -> 0 us
  between operations: 13.7 us -> 0.02 us
  other arithmetic: 8.74 us -> 0 us
    all_gather x2 -> x0, waiting for transfers between devices: 164 us -> none  [the longest x1 83.2 us: local(): key_piece = lax.all_gather(keys, 'seq', axis=0, tiled=True)]
    pallas_call x0 -> x1, Pallas kernels: none -> 52.4 us  [local(): pl.pallas_call(kernel, out_shape=jax.ShapeDtypeStruct((20, 2048), bf16),...]
    all_to_all x1 -> x0, starting transfers between devices: 20.9 us -> none  [local(): lax.all_to_all(all_frames, 'seq', split_axis=0, concat_axis=1, tiled=True)]
    all_gather x1 -> x0, blocking collectives: 19.4 us -> none  [local(): all_frames = lax.all_gather(patches, 'tile', axis=0, tiled=True)]
    unnamed x48 -> x21, local copies, waits for them, and re-layouts: 28.3 us -> 9.62 us
    dot_general x5 -> x0, matrix products: 18.5 us -> none  [the longest x1 7.06 us: local(): jnp.einsum('qhe,khe->hqk', queries, key_piece, preferred_element_type=jnp...]
    ppermute x4 -> x0, starting transfers between devices: 14.7 us -> none  [the longest x2 8.61 us: padded(): lax.ppermute(tail, axis, [(i, (i + 1) % count) for i in range(ends)])]
    all_to_all x1 -> x0, blocking collectives: 13.8 us -> none  [local(): lax.all_to_all(outputs, ('grp', 'tile'), split_axis=0, concat_axis=1, til...]
  transfers between devices with their start and end apart: 7 -> 0, of which waited for: 6 -> 0; matrix products, arithmetic and copies ran while one was open for 4% -> 0% of each run, Pallas kernels for 0% -> 0%
where the time goes in v1:
time: 63 us; the launch traced here: 62 us
  Pallas kernels  52.4 us (83%)
  local copies, waits for them, and re-layouts  9.62 us (15%)
    pallas_call x1, Pallas kernels, local(): pl.pallas_call(kernel, out_shape=jax.ShapeDtypeStruct((20, 2048), bf16),...  52.4 us
    unnamed x21, local copies, waits for them, and re-layouts  9.62 us

profile of v1, /device:TPU:1, one launch (start us, length us, event | category | flops | bytes accessed | tf_op | source)
XLA Modules:
  0.0 62.0 jit_solution(6863288122589209596)
XLA Ops:
  0.0 0.0 copy-start
  0.0 1.9 %copy-done = bf16[4096,3,1,128]{3,0,2,1:T(8,128)(2,1)S(1)} copy-done((bf16[4096,3,1,128]{3,0,2,1:T(8,128)(2,1)S(1)}, bf16[4096,3,1,128]{3,0,2,1:T(8,128)(2,1)}, u32[]{:S(2)}) %copy-start) | copy-done | bytes 3145752
  1.9 0.0 copy-start.1
  1.9 1.0 %copy-done.1 = bf16[64,4096]{1,0:T(8,128)(2,1)S(1)} copy-done((bf16[64,4096]{1,0:T(8,128)(2,1)S(1)}, bf16[64,4096]{1,0:T(8,128)(2,1)}, u32[]{:S(2)}) %copy-start.1) | copy-done | bytes 524312
  2.9 0.0 copy-start.2
  2.9 1.0 %copy-done.2 = bf16[3,3,3,512,16]{3,4,2,1,0:T(8,128)(2,1)S(1)} copy-done((bf16[3,3,3,512,16]{3,4,2,1,0:T(8,128)(2,1)S(1)}, bf16[3,3,3,512,16]{3,4,2,1,0:T(8,128)(2,1)}, u32[]{:S(2)}) %copy-start.2) | copy-done | bytes 442392
  3.9 0.0 copy-start.3
  3.9 0.9 %copy-done.3 = bf16[1,80,2,512]{3,2,1,0:T(2,128)(2,1)S(1)} copy-done((bf16[1,80,2,512]{3,2,1,0:T(2,128)(2,1)S(1)}, bf16[1,80,2,512]{3,2,1,0:T(2,128)(2,1)}, u32[]{:S(2)}) %copy-start.3) | copy-done | bytes 163864
  4.9 0.0 copy-start.4
  4.9 0.7 %copy-done.4 = f32[4096]{0:T(1024)S(1)} copy-done((f32[4096]{0:T(1024)S(1)}, f32[4096]{0:T(1024)}, u32[]{:S(2)}) %copy-start.4) | copy-done | bytes 16408
  5.6 0.0 copy-start.5
  5.6 0.7 %copy-done.5 = f32[4096]{0:T(1024)S(1)} copy-done((f32[4096]{0:T(1024)S(1)}, f32[4096]{0:T(1024)}, u32[]{:S(2)}) %copy-start.5) | copy-done | bytes 16408
  6.3 0.0 copy-start.6
  6.3 0.7 %copy-done.6 = f32[4096]{0:T(1024)S(1)} copy-done((f32[4096]{0:T(1024)S(1)}, f32[4096]{0:T(1024)}, u32[]{:S(2)}) %copy-start.6) | copy-done | bytes 16408
  7.0 0.0 copy-start.7
  7.0 0.7 %copy-done.7 = f32[16]{0:T(128)S(1)} copy-done((f32[16]{0:T(128)S(1)}, f32[16]{0:T(128)}, u32[]{:S(2)}) %copy-start.7) | copy-done | bytes 88
  7.7 0.0 copy-start.8
  7.7 0.7 %copy-done.8 = f32[128]{0:T(128)S(1)} copy-done((f32[128]{0:T(128)S(1)}, f32[128]{0:T(128)}, u32[]{:S(2)}) %copy-start.8) | copy-done | bytes 536
  8.3 0.0 copy-start.9
  8.3 0.7 %copy-done.9 = f32[128]{0:T(128)S(1)} copy-done((f32[128]{0:T(128)S(1)}, f32[128]{0:T(128)}, u32[]{:S(2)}) %copy-start.9) | copy-done | bytes 536
  9.0 52.4 %shard_map.100 = bf16[20,2048]{1,0:T(8,128)(2,1)S(1)} custom-call(bf16[80,2,512]{2,1,0:T(2,128)(2,1)S(1)} %bitcast.19, bf16[432,512]{1,0:T(8,128)(2,1)S(1)} %bitcast.18, f32[1,16]{1,0:T(1,128)S(1)} %bitcast.23, bf16[64,4096]{1,0:T(8,128)(2,1)S(1)} %copy-done.1, f32[1,4096]{1,0:T(1,128)S(1)} %bitcast.20, f32[1,4096]{1,0:T(1,128)S(1)} %bitcast.21, ...), custom_call_target="tpu_custom_call" | custom-call | flops 5000000000 | bytes 6000000 | tf_op jit(solution)/shard_map/pallas_call | solution.py:440
  61.4 0.6 %copy.13 = bf16[1,1,20,2048]{3,2,1,0:T(8,128)(2,1)} copy(bf16[1,1,20,2048]{3,2,1,0:T(8,128)(2,1)S(1)} %bitcast.16) | data formatting | bytes 163840
Async XLA Ops:
  0.0 1.9 %copy-start = (bf16[4096,3,1,128]{3,0,2,1:T(8,128)(2,1)S(1)}, bf16[4096,3,1,128]{3,0,2,1:T(8,128)(2,1)}, u32[]{:S(2)}) copy-start(bf16[4096,3,1,128]{3,0,2,1:T(8,128)(2,1)} %param.17) | copy-start | bytes 9437188
  1.9 1.0 %copy-start.1 = (bf16[64,4096]{1,0:T(8,128)(2,1)S(1)}, bf16[64,4096]{1,0:T(8,128)(2,1)}, u32[]{:S(2)}) copy-start(bf16[64,4096]{1,0:T(8,128)(2,1)} %emb_hbm.1) | copy-start | bytes 1572868
  2.9 1.0 %copy-start.2 = (bf16[3,3,3,512,16]{3,4,2,1,0:T(8,128)(2,1)S(1)}, bf16[3,3,3,512,16]{3,4,2,1,0:T(8,128)(2,1)}, u32[]{:S(2)}) copy-start(bf16[3,3,3,512,16]{3,4,2,1,0:T(8,128)(2,1)} %param.11) | copy-start | bytes 1327108
  3.9 0.9 %copy-start.3 = (bf16[1,80,2,512]{3,2,1,0:T(2,128)(2,1)S(1)}, bf16[1,80,2,512]{3,2,1,0:T(2,128)(2,1)}, u32[]{:S(2)}) copy-start(bf16[1,80,2,512]{3,2,1,0:T(2,128)(2,1)} %param.10) | copy-start | bytes 491524
  4.9 0.7 %copy-start.4 = (f32[4096]{0:T(1024)S(1)}, f32[4096]{0:T(1024)}, u32[]{:S(2)}) copy-start(f32[4096]{0:T(1024)} %param.14) | copy-start | bytes 49156
  5.6 0.7 %copy-start.5 = (f32[4096]{0:T(1024)S(1)}, f32[4096]{0:T(1024)}, u32[]{:S(2)}) copy-start(f32[4096]{0:T(1024)} %param.15) | copy-start | bytes 49156
  6.3 0.7 %copy-start.6 = (f32[4096]{0:T(1024)S(1)}, f32[4096]{0:T(1024)}, u32[]{:S(2)}) copy-start(f32[4096]{0:T(1024)} %param.16) | copy-start | bytes 49156
  7.0 0.7 %copy-start.7 = (f32[16]{0:T(128)S(1)}, f32[16]{0:T(128)}, u32[]{:S(2)}) copy-start(f32[16]{0:T(128)} %param.12) | copy-start | bytes 196
  7.7 0.7 %copy-start.8 = (f32[128]{0:T(128)S(1)}, f32[128]{0:T(128)}, u32[]{:S(2)}) copy-start(f32[128]{0:T(128)} %param.18) | copy-start | bytes 1540
  8.3 0.7 %copy-start.9 = (f32[128]{0:T(128)S(1)}, f32[128]{0:T(128)}, u32[]{:S(2)}) copy-start(f32[128]{0:T(128)} %param.19) | copy-start | bytes 1540

commit v2 on v1

--- a/solution.py
+++ b/solution.py
@@ -62,9 +62,9 @@
 
 
 def kernel(
-    x_ref, cw_ref, cbias_ref, emb_hbm, ebias_ref, shift_ref, scale_ref, w_hbm, qg_ref, kg_ref,
+    x_hbm, cw_hbm, cbias_hbm, emb_hbm, ebias_hbm, shift_hbm, scale_hbm, w_hbm, qg_hbm, kg_hbm,
     o_ref,
-    emb_ref, w_ref, halo_out, halo_in, ybuf, ysend, dens, gat, res, rr, wkv, bias_k, bias_v, gcol,
+    x_ref, cw_ref, cbias_ref, emb_ref, ebias_ref, shift_ref, scale_ref, w_ref, qg_ref, kg_ref, halo_out, halo_in, ybuf, ysend, dens, gat, res, rr, wkv, bias_k, bias_v, gcol,
     kt, vt, qscr, qrows, acc, tot, asend, arecv,
     local_sem, hs_sem, hr_sem, ys_sem, yr_sem, zs_sem, zr_sem, xs_sem, xr_sem, cs_sem, cr_sem, as_sem, ar_sem,
 ):
@@ -91,10 +91,13 @@
     halo_seq = (left, s, right)
     halo_frame = (after, f, before)
 
-    w_copy = pltpu.make_async_copy(w_hbm, w_ref, local_sem.at[0])
-    e_copy = pltpu.make_async_copy(emb_hbm, emb_ref, local_sem.at[1])
-    e_copy.start()
-    w_copy.start()
+    pairs = (
+        (x_hbm, x_ref), (cw_hbm, cw_ref), (cbias_hbm, cbias_ref), (emb_hbm, emb_ref), (ebias_hbm, ebias_ref),
+        (shift_hbm, shift_ref), (scale_hbm, scale_ref), (w_hbm, w_ref), (qg_hbm, qg_ref), (kg_hbm, kg_ref),
+    )
+    fetch = [pltpu.make_async_copy(src, dst, local_sem.at[n]) for n, (src, dst) in enumerate(pairs)]
+    for c in fetch:
+        c.start()
 
     barrier = pltpu.get_barrier_semaphore()
 
@@ -119,6 +122,8 @@
     lax.fori_loop(1, 16, greet_head, 0)
     greet(x_dev(jnp.where(g == 0, xm, xp)))
 
+    fetch[0].wait()
+    fetch[1].wait()
     sums = conv_partials(x_ref, cw_ref, g)
     for a in range(3):
         halo_out[a] = sums[:, a * 128 : (a + 1) * 128]
@@ -141,8 +146,8 @@
     for a, t in halo:
         halo_copy(a, t).start()
 
-    e_copy.wait()
-    w_copy.wait()
+    for c in fetch[2:]:
+        c.wait()
     res[...] = jnp.zeros_like(res)
     rr[...] = jnp.zeros_like(rr)
     step = 512
@@ -435,16 +440,24 @@
     enc_features, conv_weight, conv_bias, embed_weight, embed_bias, mod_shift, mod_scale, qkv_weight, q_gain, k_gain
 ):
     vmem = pl.BlockSpec(memory_space=pltpu.VMEM)
-    hbm = pl.BlockSpec(memory_space=pl.ANY)
+    hbm = pl.BlockSpec(memory_space=pltpu.HBM)
     dma = pltpu.SemaphoreType.DMA
     out = pl.pallas_call(
         kernel,
         out_shape=jax.ShapeDtypeStruct((20, 2048), bf16),
-        in_specs=[vmem, vmem, vmem, hbm, vmem, vmem, vmem, hbm, vmem, vmem],
+        in_specs=[hbm] * 10,
         out_specs=vmem,
         scratch_shapes=[
+            pltpu.VMEM((80, 2, 512), bf16),
+            pltpu.VMEM((432, 512), bf16),
+            pltpu.VMEM((1, 16), f32),
             pltpu.VMEM((64, D), bf16),
+            pltpu.VMEM((1, D), f32),
+            pltpu.VMEM((1, D), f32),
+            pltpu.VMEM((1, D), f32),
             pltpu.VMEM((3, D, 128), bf16),
+            pltpu.VMEM((1, 128), f32),
+            pltpu.VMEM((1, 128), f32),
             pltpu.VMEM((3, 24, 128), f32),
             pltpu.VMEM((3, 3, 24, 128), f32),
             pltpu.VMEM((8, 16, 128), bf16),
@@ -465,7 +478,7 @@
             pltpu.VMEM((320, 128), f32),
             pltpu.VMEM((16, 32, 128), bf16),
             pltpu.VMEM((16, 32, 128), bf16),
-            dma((2,)),
+            dma((10,)),
             dma((9,)),
             dma((9,)),
             dma((8,)),
@@ -480,7 +493,7 @@
             dma((16,)),
         ],
         compiler_params=pltpu.CompilerParams(
-            collective_id=0, has_side_effects=True, vmem_limit_bytes=48 * 1024 * 1024
+            collective_id=0, has_side_effects=True, vmem_limit_bytes=60 * 1024 * 1024
         ),
         cost_estimate=pl.CostEstimate(flops=5_000_000_000, bytes_accessed=6_000_000, transcendentals=3_300_000),
     )(

time: 63 us -> 56.5 us (0.90); the launches traced: 62 us -> 56.4 us
  local copies, waits for them, and re-layouts: 9.62 us -> 1.54 us
  Pallas kernels: 52.4 us -> 54.8 us
    unnamed x21 -> x1, local copies, waits for them, and re-layouts: 9.62 us -> 1.54 us
    pallas_call x1, Pallas kernels: 52.4 us -> 54.8 us  [local(): pl.pallas_call(kernel, out_shape=jax.ShapeDtypeStruct((20, 2048), bf16),...]
where the time goes in v2:
time: 56.5 us; the launch traced here: 56.4 us
  Pallas kernels  54.8 us (97%)
  local copies, waits for them, and re-layouts  1.54 us (3%)
    pallas_call x1, Pallas kernels, local(): pl.pallas_call(kernel, out_shape=jax.ShapeDtypeStruct((20, 2048), bf16),...  54.8 us
    unnamed x1, local copies, waits for them, and re-layouts  1.54 us

profile of v2, /device:TPU:1, one launch (start us, length us, event | category | flops | bytes accessed | tf_op | source)
XLA Modules:
  0.0 56.4 jit_solution(13999517423957968456)
XLA Ops:
  0.0 54.8 %shard_map.100 = bf16[20,2048]{1,0:T(8,128)(2,1)} custom-call(bf16[80,2,512]{2,1,0:T(2,128)(2,1)} %bitcast.19, bf16[432,512]{1,0:T(8,128)(2,1)} %bitcast.18, f32[1,16]{1,0:T(1,128)} %bitcast.23, bf16[64,4096]{1,0:T(8,128)(2,1)} %emb_hbm.1, f32[1,4096]{1,0:T(1,128)} %bitcast.20, f32[1,4096]{1,0:T(1,128)} %bitcast.21, f32[1,4096]{1,0:T(1,128)} %bitcast.22, ...), custom_call_target="tpu_custom_call" | custom-call | flops 5000000000 | bytes 6000000 | tf_op jit(solution)/shard_map/pallas_call | solution.py:445
  54.8 1.5 %copy.13 = bf16[1,1,20,2048]{3,2,1,0:T(8,128)(2,1)} copy(bf16[1,1,20,2048]{3,2,1,0:T(8,128)(2,1)} %bitcast.16) | data formatting | bytes 163840

commit v3 on v2

--- a/solution.py
+++ b/solution.py
@@ -64,9 +64,10 @@
 def kernel(
     x_hbm, cw_hbm, cbias_hbm, emb_hbm, ebias_hbm, shift_hbm, scale_hbm, w_hbm, qg_hbm, kg_hbm,
     o_ref,
-    x_ref, cw_ref, cbias_ref, emb_ref, ebias_ref, shift_ref, scale_ref, w_ref, qg_ref, kg_ref, halo_out, halo_in, ybuf, ysend, dens, gat, res, rr, wkv, bias_k, bias_v, gcol,
-    kt, vt, qscr, qrows, acc, tot, asend, arecv,
-    local_sem, hs_sem, hr_sem, ys_sem, yr_sem, zs_sem, zr_sem, xs_sem, xr_sem, cs_sem, cr_sem, as_sem, ar_sem,
+    x_ref, cw_ref, cbias_ref, emb_ref, ebias_ref, shift_ref, scale_ref, w_ref, qg_ref, kg_ref, halo_out, halo_in, ybuf, ysend, dens, gat, qbuf, res, rr, wkv, wv, bias_k, gcol,
+    kt, vt, qrows, acc, asend, arecv,
+    local_sem, hs_sem, hr_sem, ys_sem, yr_sem, qs_sem, qr_sem, qc_sem, zs_sem, zr_sem, xs_sem, xr_sem, cs_sem, cr_sem,
+    as_sem, ar_sem,
 ):
     g = lax.axis_index("grp")
     s = lax.axis_index("seq")
@@ -120,7 +121,21 @@
         return 0
 
     lax.fori_loop(1, 16, greet_head, 0)
+    greet(x_dev(xo))
     greet(x_dev(jnp.where(g == 0, xm, xp)))
+
+    def greet_q(i, _):
+        zz = lax.rem(z + i, 8)
+        for hx in range(2):
+            owner = hx * 2 + z % 2
+
+            @pl.when(owner != x)
+            def _():
+                greet((owner % 2, hx * 16 + zz * 2 + core, f))
+
+        return 0
+
+    lax.fori_loop(1, 8, greet_q, 0)
 
     fetch[0].wait()
     fetch[1].wait()
@@ -129,7 +144,7 @@
         halo_out[a] = sums[:, a * 128 : (a + 1) * 128]
     halo_in[1, 1] = sums[:, 128:256]
 
-    pl.semaphore_wait(barrier, 29)
+    pl.semaphore_wait(barrier, 30 + jnp.where(z % 2 == g, 9, 12))
 
     def halo_copy(a, t):
         n = a * 3 + t
@@ -175,11 +190,19 @@
     lane = lax.broadcasted_iota(jnp.int32, (128, 128), 1)
     row = lax.broadcasted_iota(jnp.int32, (128, 128), 0)
     low = lane < 64
-    zero64 = jnp.zeros((64, 128), f32)
     for j in range(3):
         cols = slice(j * 128, (j + 1) * 128)
         top = res[0:64, cols] + res[64:128, cols]
         rest = res[128:136, cols] + res[136:144, cols]
+        if j == 2:
+            row8 = lax.broadcasted_iota(jnp.int32, (8, 128), 0)
+            rest = jnp.where(row8 == 2, rest[0:1, :], rest)
+            m = jnp.concatenate([top, rest, jnp.zeros((56, 128), f32)], axis=0)
+            hi, lo = hi_lo(m)
+            wv[0:128] = hi
+            wv[128:256] = hi
+            wv[256:384] = lo
+            continue
         m = jnp.concatenate([top, rest, jnp.zeros((56, 128), f32)], axis=0)
         mt = m.T
         a_t = jnp.where(low, mt, 0.0)
@@ -189,18 +212,17 @@
             n = (j * 2 + half) * 128
             wkv[n : n + 128, 0:128] = hi
             wkv[n : n + 128, 128:256] = lo
-        if j > 0:
-            bias_v_ref = bias_k if j == 1 else bias_v
-            bias_v_ref[0] = jnp.broadcast_to(mt[:, 64:65], (128, 128))
-            bias_v_ref[1] = jnp.broadcast_to(mt[:, 65:66], (128, 128))
+        if j == 1:
+            bias_k[0] = jnp.broadcast_to(mt[:, 64:65], (128, 128))
+            bias_k[1] = jnp.broadcast_to(mt[:, 65:66], (128, 128))
     gram = rr[...]
     g_t = jnp.where(low & (row < 64), gram, 0.0)
     gblock = g_t + pltpu.roll(pltpu.roll(g_t, 64, 1), 64, 0)
     hi, lo = hi_lo(gblock)
-    wkv[768:896, 0:128] = hi
-    wkv[768:896, 128:256] = lo
-    wkv[896:1024, 0:128] = jnp.where(lane == row, 1.0, 0.0).astype(bf16)
-    wkv[896:1024, 128:256] = jnp.zeros((128, 128), bf16)
+    wkv[512:640, 0:128] = hi
+    wkv[512:640, 128:256] = lo
+    wkv[640:768, 0:128] = jnp.where(lane == row, 1.0, 0.0).astype(bf16)
+    wkv[640:768, 128:256] = jnp.zeros((128, 128), bf16)
     grow = gram[64:65, :] + gram[65:66, :]
     lane1 = lax.broadcasted_iota(jnp.int32, (1, 128), 1)
     bb = jnp.sum(jnp.where((lane1 == 64) | (lane1 == 65), grow, 0.0), axis=1, keepdims=True)
@@ -209,6 +231,8 @@
     gc = gram[:, 64:65] + gram[:, 65:66]
     gc2 = 2.0 * jnp.broadcast_to(jnp.concatenate([gc[0:64], gc[0:64]], axis=0), (128, 128))
     gcol[...] = gc2
+    vt[64:128, :] = jnp.zeros((64, 10240), bf16)
+    acc[...] = jnp.zeros_like(acc)
 
     for a, t in halo:
         halo_copy(a, t).wait_recv()
@@ -259,107 +283,151 @@
         y_arrived(i).wait_recv()
     for n in range(8):
         dens[n * 10 : n * 10 + 10, :] = ybuf[n, 0:10, :].astype(f32)
-    gat[x, core, z] = dens[...].astype(bf16)
+    gat[z, x, core] = dens[...].astype(bf16)
+
+    def q_copy(xq, k):
+        zq = 2 * k + g
+        return pltpu.make_async_remote_copy(
+            src_ref=ybuf.at[4 * (xq // 2) + k], dst_ref=qbuf.at[core, xh * 8 + z], send_sem=qs_sem.at[xq * 4 + k],
+            recv_sem=qr_sem.at[xh * 8 + z], device_id=(xq % 2, (xq // 2) * 16 + zq * 2 + core, f),
+            device_id_type=pl.DeviceIdType.MESH,
+        )
+
+    def q_away(xq, k):
+        return (x != xq) | (z != 2 * k + g)
+
+    for xq in range(4):
+        for k in range(4):
+
+            @pl.when(q_away(xq, k))
+            def _():
+                q_copy(xq, k).start()
+
+    @pl.when(z % 2 == g)
+    def _():
+        pltpu.make_async_copy(
+            ybuf.at[4 * xh + z // 2], qbuf.at[core, xh * 8 + z], qr_sem.at[xh * 8 + z]
+        ).start()
+
+    steps = (0, 1, 7, 2, 6, 3, 5, 4)
+
+    def at(n):
+        return lax.rem(z + steps[n], 8)
 
     def z_copy(i, zz):
         return pltpu.make_async_remote_copy(
-            src_ref=gat.at[x, core, z], dst_ref=gat.at[x, core, z], send_sem=zs_sem.at[i], recv_sem=zr_sem.at[i],
+            src_ref=gat.at[z, x, core], dst_ref=gat.at[z, x, core], send_sem=zs_sem.at[i], recv_sem=zr_sem.at[i],
             device_id=z_dev(zz), device_id_type=pl.DeviceIdType.MESH,
         )
 
-    def z_arrived(i, zz):
-        return pltpu.make_async_remote_copy(
-            src_ref=gat.at[x, core, z], dst_ref=gat.at[x, core, zz], send_sem=zs_sem.at[i], recv_sem=zr_sem.at[i],
-            device_id=z_dev(zz), device_id_type=pl.DeviceIdType.MESH,
-        )
-
-    for i in (1, 7, 2, 6, 3, 5, 4):
-        z_copy(i, lax.rem(z + i, 8)).start()
-    for i in (1, 7, 2, 6, 3, 5, 4):
-        z_arrived(i, lax.rem(z + 8 - i, 8)).wait_recv()
-
-    def chunk(xx, cc, part):
-        ref = gat.at[xx, cc]
-        if part == 0:
-            return ref
-        return ref.at[pl.ds((part - 1) * 4, 4)]
-
-    def x_copy(n, xx, part, to):
-        return pltpu.make_async_remote_copy(
-            src_ref=chunk(xx, core, part), dst_ref=chunk(xx, core, part), send_sem=xs_sem.at[n],
-            recv_sem=xr_sem.at[n], device_id=x_dev(to), device_id_type=pl.DeviceIdType.MESH,
-        )
-
-    def c_copy(n, xx, part, cc):
-        return pltpu.make_async_remote_copy(
-            src_ref=chunk(xx, cc, part), dst_ref=chunk(xx, cc, part), send_sem=cs_sem.at[n],
-            recv_sem=cr_sem.at[n], device_id=partner, device_id_type=pl.DeviceIdType.MESH,
-        )
-
-    def keys(xx, cc):
-        rows = gat[xx, cc].reshape(640, 128)
+    def z_arrived(n):
+        i = 8 - steps[n]
+        return pltpu.make_async_remote_copy(
+            src_ref=gat.at[z, x, core], dst_ref=gat.at[at(n), x, core], send_sem=zs_sem.at[i], recv_sem=zr_sem.at[i],
+            device_id=z_dev(at(n)), device_id_type=pl.DeviceIdType.MESH,
+        )
+
+    def x_copy(n, d):
+        piece = gat.at[at(n), x, core]
+        return pltpu.make_async_remote_copy(
+            src_ref=piece, dst_ref=piece, send_sem=xs_sem.at[n, d], recv_sem=xr_sem.at[at(n), d],
+            device_id=x_dev(lax.rem(x + d, 4)), device_id_type=pl.DeviceIdType.MESH,
+        )
+
+    def x_arrived(n, d):
+        xx = lax.rem(x + 4 - d, 4)
+        piece = gat.at[at(n), xx, core]
+        return pltpu.make_async_remote_copy(
+            src_ref=piece, dst_ref=piece, send_sem=xs_sem.at[n, d], recv_sem=xr_sem.at[at(n), d],
+            device_id=x_dev(xx), device_id_type=pl.DeviceIdType.MESH,
+        )
+
+    def c_copy(n, d, cc):
+        xx = lax.rem(x + d, 4)
+        piece = gat.at[at(n), xx, cc]
+        return pltpu.make_async_remote_copy(
+            src_ref=piece, dst_ref=piece, send_sem=cs_sem.at[n, d], recv_sem=cr_sem.at[n, d],
+            device_id=partner, device_id_type=pl.DeviceIdType.MESH,
+        )
+
+    def spread(n):
+        if n > 0:
+            z_arrived(n).wait_recv()
+        for d in (2, 1, 3):
+            x_copy(n, d).start()
+        c_copy(n, 0, core).start()
+
+    def share(n):
+        for d in (1, 3, 2):
+            x_arrived(n, d).wait_recv()
+            c_copy(n, 4 - d, core).start()
+
+    def complete(n):
+        for d in range(4):
+            c_copy(n, d, 1 - core).wait_recv()
+
+    def keys(m):
+        rows = jnp.concatenate([gat[at(n)].reshape(640, 128) for n in (2 * m, 2 * m + 1)], axis=0)
         p2 = jnp.concatenate([rows, rows], axis=1)
-        out = nt_dot(wkv[256:1024, :], p2)
-        y = (out[512:640] + jnp.concatenate([gcol[...]] * 5, axis=1)) * out[640:768]
-        base = pl.multiple_of((xx * 2 + cc) * 1280, 1280)
+        out = nt_dot(wkv[256:768, :], p2)
+        pt = out[384:512]
+        y = (out[256:384] + jnp.concatenate([gcol[...]] * 10, axis=1)) * pt
+        row8 = lax.broadcasted_iota(jnp.int32, (16, 1280), 0)
         for half in range(2):
             ms = jnp.sum(y[half * 64 : half * 64 + 64], axis=0, keepdims=True) + bb
             inv = lax.rsqrt(jnp.maximum(ms, 0.0) * (1.0 / D) + EPS)
             kr = out[half * 128 : half * 128 + 128]
-            kr = (kr + jnp.concatenate([bias_k[0]] * 5, axis=1)) * inv + jnp.concatenate([bias_k[1]] * 5, axis=1)
+            kr = (kr + jnp.concatenate([bias_k[0]] * 10, axis=1)) * inv + jnp.concatenate([bias_k[1]] * 10, axis=1)
             ks = lax.rsqrt(jnp.sum(kr * kr, axis=0, keepdims=True) * (1.0 / 128) + EPS)
-            cols = pl.ds(base + half * 640, 640)
+            cols = slice(m * 2560 + half * 1280, m * 2560 + half * 1280 + 1280)
             kt[:, cols] = (kr * ks).astype(bf16)
-            vr = out[256 + half * 128 : 256 + half * 128 + 128]
-            vr = (vr + jnp.concatenate([bias_v[0]] * 5, axis=1)) * inv + jnp.concatenate([bias_v[1]] * 5, axis=1)
-            vt[:, cols] = vr.astype(bf16)
-
-    other = 1 - core
-    x_copy(0, x, 0, xp).start()
-    x_copy(1, x, 0, xm).start()
-    c_copy(0, x, 0, core).start()
-    keys(x, core)
-    c_copy(0, x, 0, other).wait_recv()
-    keys(x, other)
-    x_copy(0, xm, 0, xp).wait_recv()
-    x_copy(2, xm, 1, xp).start()
-    c_copy(1, xm, 0, core).start()
-    x_copy(1, xp, 0, xm).wait_recv()
-    x_copy(3, xp, 2, xm).start()
-    c_copy(2, xp, 0, core).start()
-    keys(xm, core)
-    keys(xp, core)
-    c_copy(1, xm, 0, other).wait_recv()
-    keys(xm, other)
-    c_copy(2, xp, 0, other).wait_recv()
-    keys(xp, other)
-    x_copy(2, xo, 1, xp).wait_recv()
-    c_copy(3, xo, 1, core).start()
-    x_copy(3, xo, 2, xm).wait_recv()
-    c_copy(4, xo, 2, core).start()
-    keys(xo, core)
-    c_copy(3, xo, 1, other).wait_recv()
-    c_copy(4, xo, 2, other).wait_recv()
-    keys(xo, other)
-
-    fq, gq, hq = s // 4, (s // 2) % 2, s % 2
-    pick_row = lax.broadcasted_iota(jnp.int32, (16, 80), 0)
-    pick_col = lax.broadcasted_iota(jnp.int32, (16, 80), 1)
-    pick = jnp.where((pick_row < 10) & (pick_col == pick_row + fq * 10), 1.0, 0.0).astype(bf16)
-    for hx in range(2):
-        blocks = [gat[hx * 2 + gq, cc, zz] for zz in range(8) for cc in range(2)]
-        picked = jnp.dot(pick, jnp.concatenate(blocks, axis=1), preferred_element_type=f32)
-        for n in range(16):
-            qscr[hx * 16 + n] = picked[:, n * 128 : (n + 1) * 128]
-    qall = qscr[...]
-    for i in range(10):
-        qrows[i * 32 : (i + 1) * 32, :] = qall[:, i, :]
+            vt[0:64, cols] = (pt[half * 64 : half * 64 + 64] * inv).astype(bf16)
+            inv_hi = inv.astype(bf16).astype(f32)
+            extra = jnp.where(row8 == 0, inv_hi, jnp.where(row8 == 1, 1.0, jnp.where(row8 == 2, inv - inv_hi, 0.0)))
+            vt[64:80, cols] = extra.astype(bf16)
+
+    def attend(m):
+        cols = slice(m * 2560, m * 2560 + 2560)
+        w = jnp.exp2(jnp.dot(q, kt[:, cols], preferred_element_type=f32))
+        acc[...] += nt_dot(w.astype(bf16), vt[:, cols])
+
+    for i in (1, 7, 2, 6, 3, 5, 4):
+        z_copy(i, lax.rem(z + i, 8)).start()
+    spread(0)
+    spread(1)
+    spread(2)
+    share(0)
+    spread(3)
+    spread(4)
+    for n in range(16):
+        pltpu.make_async_copy(ybuf.at[0], qbuf.at[core, n], qr_sem.at[n]).wait()
+
+    def q_share(cc):
+        return pltpu.make_async_remote_copy(
+            src_ref=qbuf.at[cc], dst_ref=qbuf.at[cc], send_sem=qc_sem.at[0], recv_sem=qc_sem.at[1],
+            device_id=partner, device_id_type=pl.DeviceIdType.MESH,
+        )
+
+    q_share(core).start()
+    spread(5)
+    spread(6)
+    spread(7)
+    share(1)
+    complete(0)
+    complete(1)
+    keys(0)
+    q_share(1 - core).wait_recv()
+    hq = core
+    for cc in range(2):
+        qall = qbuf[cc].astype(f32)
+        for i in range(10):
+            qrows[pl.ds(i * 32 + cc, 16, stride=2), :] = qall[:, i, :]
     qp = qrows[...]
     qb = qp.astype(bf16)
     q2 = jnp.concatenate([qb, qb], axis=1)
     wq = jnp.where(hq == 0, wkv[0:128, :].astype(f32), wkv[128:256, :].astype(f32)).astype(bf16)
     raw = nt_dot(q2, wq)
-    gp = nt_dot(q2, wkv[768:896, :])
+    gp = nt_dot(q2, wkv[512:640, :])
     lane320 = lax.broadcasted_iota(jnp.int32, (320, 128), 1)
     y = jnp.where(lane320 // 64 == hq, (gp + grow2) * qp, 0.0)
     ms = jnp.sum(y, axis=1, keepdims=True) + bb
@@ -369,23 +437,29 @@
     qr = (raw + c_q) * inv + d_q
     qs = lax.rsqrt(jnp.sum(qr * qr, axis=1, keepdims=True) * (1.0 / 128) + EPS)
     q = (qr * qs * (qg_ref[...] * kg_ref[...] * (math.log2(math.e) / math.sqrt(128.0)))).astype(bf16)
-
-    acc[...] = jnp.zeros_like(acc)
-    tot[...] = jnp.zeros_like(tot)
-    width = 2560
-
-    def attend(n, _):
-        cols = pl.ds(pl.multiple_of(n * width, width), width)
-        w = jnp.exp2(jnp.dot(q, kt[:, cols], preferred_element_type=f32))
-        t = w[:, 0:128]
-        for m in range(1, width // 128):
-            t = t + w[:, m * 128 : (m + 1) * 128]
-        tot[...] += t
-        acc[...] += nt_dot(w.astype(bf16), vt[:, cols])
-        return 0
-
-    lax.fori_loop(0, 10240 // width, attend, 0)
-    out = acc[...] / jnp.sum(tot[...], axis=1, keepdims=True)
+    share(2)
+    share(3)
+    attend(0)
+    share(4)
+    share(5)
+    complete(2)
+    complete(3)
+    keys(1)
+    attend(1)
+    share(6)
+    share(7)
+    complete(4)
+    complete(5)
+    keys(2)
+    attend(2)
+    complete(6)
+    complete(7)
+    keys(3)
+    attend(3)
+    u = acc[...]
+    hi, lo = hi_lo(u)
+    numer = jnp.dot(jnp.concatenate([hi, lo, hi], axis=1), wv[...], preferred_element_type=f32)
+    out = numer / u[:, 65:66]
     pad = jnp.zeros((12, 128), f32)
     for j in range(16):
         asend[j] = jnp.concatenate([out[j * 20 : j * 20 + 20], pad], axis=0).astype(bf16)
@@ -409,15 +483,19 @@
     for i in range(1, 8):
         y_copy(i).wait_send()
         z_copy(i, lax.rem(z + i, 8)).wait_send()
-    x_copy(0, x, 0, xp).wait_send()
-    x_copy(1, x, 0, xm).wait_send()
-    x_copy(2, xm, 1, xp).wait_send()
-    x_copy(3, xp, 2, xm).wait_send()
-    c_copy(0, x, 0, core).wait_send()
-    c_copy(1, xm, 0, core).wait_send()
-    c_copy(2, xp, 0, core).wait_send()
-    c_copy(3, xo, 1, core).wait_send()
-    c_copy(4, xo, 2, core).wait_send()
+    for xq in range(4):
+        for k in range(4):
+
+            @pl.when(q_away(xq, k))
+            def _():
+                q_copy(xq, k).wait_send()
+
+    q_share(core).wait_send()
+    for n in range(8):
+        for d in range(1, 4):
+            x_copy(n, d).wait_send()
+        for d in range(4):
+            c_copy(n, d, core).wait_send()
 
     def head_arrived(i, _):
         j = lax.rem(head + 16 - i, 16)
@@ -463,17 +541,16 @@
             pltpu.VMEM((8, 16, 128), bf16),
             pltpu.VMEM((16, 128), bf16),
             pltpu.VMEM((80, 128), f32),
-            pltpu.VMEM((4, 2, 8, 80, 128), bf16),
+            pltpu.VMEM((8, 4, 2, 80, 128), bf16),
+            pltpu.VMEM((2, 16, 16, 128), bf16),
             pltpu.VMEM((144, 384), f32),
             pltpu.VMEM((128, 128), f32),
-            pltpu.VMEM((1024, 256), bf16),
-            pltpu.VMEM((2, 128, 128), f32),
+            pltpu.VMEM((768, 256), bf16),
+            pltpu.VMEM((384, 128), bf16),
             pltpu.VMEM((2, 128, 128), f32),
             pltpu.VMEM((128, 128), f32),
             pltpu.VMEM((128, 10240), bf16),
             pltpu.VMEM((128, 10240), bf16),
-            pltpu.VMEM((32, 16, 128), f32),
-            pltpu.VMEM((320, 128), f32),
             pltpu.VMEM((320, 128), f32),
             pltpu.VMEM((320, 128), f32),
             pltpu.VMEM((16, 32, 128), bf16),
@@ -483,12 +560,15 @@
             dma((9,)),
             dma((8,)),
             dma((8,)),
+            dma((16,)),
+            dma((16,)),
+            dma((2,)),
             dma((8,)),
             dma((8,)),
-            dma((4,)),
-            dma((4,)),
-            dma((5,)),
-            dma((5,)),
+            dma((8, 4)),
+            dma((8, 4)),
+            dma((8, 4)),
+            dma((8, 4)),
             dma((16,)),
             dma((16,)),
         ],

time: 56.5 us -> 54.6 us (0.966)
  Pallas kernels: 54.8 us -> 52.9 us
    pallas_call x1, Pallas kernels: 54.8 us -> 52.9 us  [local(): pl.pallas_call(kernel, out_shape=jax.ShapeDtypeStruct((20, 2048), bf16),...]
where the time goes in v3:
time: 54.6 us; the launch traced here: 54.5 us
  Pallas kernels  52.9 us (97%)
  local copies, waits for them, and re-layouts  1.54 us (3%)
    pallas_call x1, Pallas kernels, local(): pl.pallas_call(kernel, out_shape=jax.ShapeDtypeStruct((20, 2048), bf16),...  52.9 us
    unnamed x1, local copies, waits for them, and re-layouts  1.54 us

profile of v3, /device:TPU:1, one launch (start us, length us, event | category | flops | bytes accessed | tf_op | source)
XLA Modules:
  0.0 54.5 jit_solution(873927829534852063)
XLA Ops:
  0.0 52.9 %shard_map.100 = bf16[20,2048]{1,0:T(8,128)(2,1)} custom-call(bf16[80,2,512]{2,1,0:T(2,128)(2,1)} %bitcast.19, bf16[432,512]{1,0:T(8,128)(2,1)} %bitcast.18, f32[1,16]{1,0:T(1,128)} %bitcast.23, bf16[64,4096]{1,0:T(8,128)(2,1)} %emb_hbm.1, f32[1,4096]{1,0:T(1,128)} %bitcast.20, f32[1,4096]{1,0:T(1,128)} %bitcast.21, f32[1,4096]{1,0:T(1,128)} %bitcast.22, ...), custom_call_target="tpu_custom_call" | custom-call | flops 5000000000 | bytes 6000000 | tf_op jit(solution)/shard_map/pallas_call | solution.py:523
  52.9 1.5 %copy.13 = bf16[1,1,20,2048]{3,2,1,0:T(8,128)(2,1)} copy(bf16[1,1,20,2048]{3,2,1,0:T(8,128)(2,1)} %bitcast.16) | data formatting | bytes 163840

commit v4 on v3

--- a/solution.py
+++ b/solution.py
@@ -64,9 +64,9 @@
 def kernel(
     x_hbm, cw_hbm, cbias_hbm, emb_hbm, ebias_hbm, shift_hbm, scale_hbm, w_hbm, qg_hbm, kg_hbm,
     o_ref,
-    x_ref, cw_ref, cbias_ref, emb_ref, ebias_ref, shift_ref, scale_ref, w_ref, qg_ref, kg_ref, halo_out, halo_in, ybuf, ysend, dens, gat, qbuf, res, rr, wkv, wv, bias_k, gcol,
-    kt, vt, qrows, acc, asend, arecv,
-    local_sem, hs_sem, hr_sem, ys_sem, yr_sem, qs_sem, qr_sem, qc_sem, zs_sem, zr_sem, xs_sem, xr_sem, cs_sem, cr_sem,
+    x_ref, cw_ref, cbias_ref, emb_ref, ebias_ref, shift_ref, scale_ref, w_ref, qg_ref, kg_ref, halo_out, halo_in, ybuf, ysend, dens, gat, res, rr, wkv, wv, bias_k, gcol,
+    kt, vt, qscr, qrows, acc, asend, arecv,
+    local_sem, hs_sem, hr_sem, ys_sem, yr_sem, zs_sem, zr_sem, xs_sem, xr_sem, cs_sem, cr_sem,
     as_sem, ar_sem,
 ):
     g = lax.axis_index("grp")
@@ -97,8 +97,8 @@
         (shift_hbm, shift_ref), (scale_hbm, scale_ref), (w_hbm, w_ref), (qg_hbm, qg_ref), (kg_hbm, kg_ref),
     )
     fetch = [pltpu.make_async_copy(src, dst, local_sem.at[n]) for n, (src, dst) in enumerate(pairs)]
-    for c in fetch:
-        c.start()
+    fetch[0].start()
+    fetch[1].start()
 
     barrier = pltpu.get_barrier_semaphore()
 
@@ -124,19 +124,8 @@
     greet(x_dev(xo))
     greet(x_dev(jnp.where(g == 0, xm, xp)))
 
-    def greet_q(i, _):
-        zz = lax.rem(z + i, 8)
-        for hx in range(2):
-            owner = hx * 2 + z % 2
-
-            @pl.when(owner != x)
-            def _():
-                greet((owner % 2, hx * 16 + zz * 2 + core, f))
-
-        return 0
-
-    lax.fori_loop(1, 8, greet_q, 0)
-
+    for c in fetch[2:]:
+        c.start()
     fetch[0].wait()
     fetch[1].wait()
     sums = conv_partials(x_ref, cw_ref, g)
@@ -144,7 +133,7 @@
         halo_out[a] = sums[:, a * 128 : (a + 1) * 128]
     halo_in[1, 1] = sums[:, 128:256]
 
-    pl.semaphore_wait(barrier, 30 + jnp.where(z % 2 == g, 9, 12))
+    pl.semaphore_wait(barrier, 30)
 
     def halo_copy(a, t):
         n = a * 3 + t
@@ -285,34 +274,10 @@
         dens[n * 10 : n * 10 + 10, :] = ybuf[n, 0:10, :].astype(f32)
     gat[z, x, core] = dens[...].astype(bf16)
 
-    def q_copy(xq, k):
-        zq = 2 * k + g
-        return pltpu.make_async_remote_copy(
-            src_ref=ybuf.at[4 * (xq // 2) + k], dst_ref=qbuf.at[core, xh * 8 + z], send_sem=qs_sem.at[xq * 4 + k],
-            recv_sem=qr_sem.at[xh * 8 + z], device_id=(xq % 2, (xq // 2) * 16 + zq * 2 + core, f),
-            device_id_type=pl.DeviceIdType.MESH,
-        )
-
-    def q_away(xq, k):
-        return (x != xq) | (z != 2 * k + g)
-
-    for xq in range(4):
-        for k in range(4):
-
-            @pl.when(q_away(xq, k))
-            def _():
-                q_copy(xq, k).start()
-
-    @pl.when(z % 2 == g)
-    def _():
-        pltpu.make_async_copy(
-            ybuf.at[4 * xh + z // 2], qbuf.at[core, xh * 8 + z], qr_sem.at[xh * 8 + z]
-        ).start()
-
-    steps = (0, 1, 7, 2, 6, 3, 5, 4)
-
     def at(n):
-        return lax.rem(z + steps[n], 8)
+        if n == 0:
+            return z
+        return jnp.where(z > n - 1, n - 1, n)
 
     def z_copy(i, zz):
         return pltpu.make_async_remote_copy(
@@ -321,7 +286,7 @@
         )
 
     def z_arrived(n):
-        i = 8 - steps[n]
+        i = lax.rem(z + 8 - at(n), 8)
         return pltpu.make_async_remote_copy(
             src_ref=gat.at[z, x, core], dst_ref=gat.at[at(n), x, core], send_sem=zs_sem.at[i], recv_sem=zr_sem.at[i],
             device_id=z_dev(at(n)), device_id_type=pl.DeviceIdType.MESH,
@@ -366,62 +331,73 @@
         for d in range(4):
             c_copy(n, d, 1 - core).wait_recv()
 
-    def keys(m):
-        rows = jnp.concatenate([gat[at(n)].reshape(640, 128) for n in (2 * m, 2 * m + 1)], axis=0)
+    def keys(*pieces):
+        rows = jnp.concatenate([gat[at(n)].reshape(640, 128) for n in pieces], axis=0)
+        size = 640 * len(pieces)
+        wide = size // 128
         p2 = jnp.concatenate([rows, rows], axis=1)
         out = nt_dot(wkv[256:768, :], p2)
         pt = out[384:512]
-        y = (out[256:384] + jnp.concatenate([gcol[...]] * 10, axis=1)) * pt
-        row8 = lax.broadcasted_iota(jnp.int32, (16, 1280), 0)
+        y = (out[256:384] + jnp.concatenate([gcol[...]] * wide, axis=1)) * pt
+        row16 = lax.broadcasted_iota(jnp.int32, (16, size), 0)
         for half in range(2):
             ms = jnp.sum(y[half * 64 : half * 64 + 64], axis=0, keepdims=True) + bb
             inv = lax.rsqrt(jnp.maximum(ms, 0.0) * (1.0 / D) + EPS)
             kr = out[half * 128 : half * 128 + 128]
-            kr = (kr + jnp.concatenate([bias_k[0]] * 10, axis=1)) * inv + jnp.concatenate([bias_k[1]] * 10, axis=1)
+            kr = (kr + jnp.concatenate([bias_k[0]] * wide, axis=1)) * inv + jnp.concatenate([bias_k[1]] * wide, axis=1)
             ks = lax.rsqrt(jnp.sum(kr * kr, axis=0, keepdims=True) * (1.0 / 128) + EPS)
-            cols = slice(m * 2560 + half * 1280, m * 2560 + half * 1280 + 1280)
+            first = pieces[0] * 1280 + half * size
+            cols = slice(first, first + size)
             kt[:, cols] = (kr * ks).astype(bf16)
             vt[0:64, cols] = (pt[half * 64 : half * 64 + 64] * inv).astype(bf16)
             inv_hi = inv.astype(bf16).astype(f32)
-            extra = jnp.where(row8 == 0, inv_hi, jnp.where(row8 == 1, 1.0, jnp.where(row8 == 2, inv - inv_hi, 0.0)))
+            extra = jnp.where(row16 == 0, inv_hi, jnp.where(row16 == 1, 1.0, jnp.where(row16 == 2, inv - inv_hi, 0.0)))
             vt[64:80, cols] = extra.astype(bf16)
 
-    def attend(m):
-        cols = slice(m * 2560, m * 2560 + 2560)
+    def attend(*pieces):
+        cols = slice(pieces[0] * 1280, pieces[-1] * 1280 + 1280)
         w = jnp.exp2(jnp.dot(q, kt[:, cols], preferred_element_type=f32))
         acc[...] += nt_dot(w.astype(bf16), vt[:, cols])
 
     for i in (1, 7, 2, 6, 3, 5, 4):
         z_copy(i, lax.rem(z + i, 8)).start()
     spread(0)
-    spread(1)
-    spread(2)
+    for n in range(1, 8):
+        spread(n)
     share(0)
-    spread(3)
-    spread(4)
-    for n in range(16):
-        pltpu.make_async_copy(ybuf.at[0], qbuf.at[core, n], qr_sem.at[n]).wait()
-
-    def q_share(cc):
-        return pltpu.make_async_remote_copy(
-            src_ref=qbuf.at[cc], dst_ref=qbuf.at[cc], send_sem=qc_sem.at[0], recv_sem=qc_sem.at[1],
-            device_id=partner, device_id_type=pl.DeviceIdType.MESH,
-        )
-
-    q_share(core).start()
-    spread(5)
-    spread(6)
-    spread(7)
     share(1)
+    share(2)
     complete(0)
+    keys(0)
+    share(3)
     complete(1)
-    keys(0)
-    q_share(1 - core).wait_recv()
-    hq = core
-    for cc in range(2):
-        qall = qbuf[cc].astype(f32)
-        for i in range(10):
-            qrows[pl.ds(i * 32 + cc, 16, stride=2), :] = qall[:, i, :]
+    keys(1)
+    share(4)
+    complete(2)
+    keys(2)
+    share(5)
+    complete(3)
+    keys(3)
+    share(6)
+    complete(4)
+    keys(4)
+    share(7)
+    complete(5)
+    complete(6)
+    keys(5, 6)
+    complete(7)
+    fq, gq, hq = s // 4, z % 2, core
+    pick_row = lax.broadcasted_iota(jnp.int32, (16, 80), 0)
+    pick_col = lax.broadcasted_iota(jnp.int32, (16, 80), 1)
+    pick = jnp.where((pick_row < 10) & (pick_col == pick_row + fq * 10), 1.0, 0.0).astype(bf16)
+    for hx in range(2):
+        blocks = [gat[zz, hx * 2 + gq, cc] for zz in range(8) for cc in range(2)]
+        picked = jnp.dot(pick, jnp.concatenate(blocks, axis=1), preferred_element_type=f32)
+        for n in range(16):
+            qscr[hx * 16 + n] = picked[:, n * 128 : (n + 1) * 128]
+    qall = qscr[...]
+    for i in range(10):
+        qrows[i * 32 : (i + 1) * 32, :] = qall[:, i, :]
     qp = qrows[...]
     qb = qp.astype(bf16)
     q2 = jnp.concatenate([qb, qb], axis=1)
@@ -437,25 +413,11 @@
     qr = (raw + c_q) * inv + d_q
     qs = lax.rsqrt(jnp.sum(qr * qr, axis=1, keepdims=True) * (1.0 / 128) + EPS)
     q = (qr * qs * (qg_ref[...] * kg_ref[...] * (math.log2(math.e) / math.sqrt(128.0)))).astype(bf16)
-    share(2)
-    share(3)
-    attend(0)
-    share(4)
-    share(5)
-    complete(2)
-    complete(3)
-    keys(1)
-    attend(1)
-    share(6)
-    share(7)
-    complete(4)
-    complete(5)
-    keys(2)
-    attend(2)
-    complete(6)
-    complete(7)
-    keys(3)
-    attend(3)
+    attend(0, 1)
+    attend(2, 3)
+    keys(7)
+    attend(4, 5)
+    attend(6, 7)
     u = acc[...]
     hi, lo = hi_lo(u)
     numer = jnp.dot(jnp.concatenate([hi, lo, hi], axis=1), wv[...], preferred_element_type=f32)
@@ -483,14 +445,6 @@
     for i in range(1, 8):
         y_copy(i).wait_send()
         z_copy(i, lax.rem(z + i, 8)).wait_send()
-    for xq in range(4):
-        for k in range(4):
-
-            @pl.when(q_away(xq, k))
-            def _():
-                q_copy(xq, k).wait_send()
-
-    q_share(core).wait_send()
     for n in range(8):
         for d in range(1, 4):
             x_copy(n, d).wait_send()
@@ -542,7 +496,6 @@
             pltpu.VMEM((16, 128), bf16),
             pltpu.VMEM((80, 128), f32),
             pltpu.VMEM((8, 4, 2, 80, 128), bf16),
-            pltpu.VMEM((2, 16, 16, 128), bf16),
             pltpu.VMEM((144, 384), f32),
             pltpu.VMEM((128, 128), f32),
             pltpu.VMEM((768, 256), bf16),
@@ -551,6 +504,7 @@
             pltpu.VMEM((128, 128), f32),
             pltpu.VMEM((128, 10240), bf16),
             pltpu.VMEM((128, 10240), bf16),
+            pltpu.VMEM((32, 16, 128), f32),
             pltpu.VMEM((320, 128), f32),
             pltpu.VMEM((320, 128), f32),
             pltpu.VMEM((16, 32, 128), bf16),
@@ -560,9 +514,6 @@
             dma((9,)),
             dma((8,)),
             dma((8,)),
-            dma((16,)),
-            dma((16,)),
-            dma((2,)),
             dma((8,)),
             dma((8,)),
             dma((8, 4)),

time: 54.6 us -> 52.1 us (0.954)
  Pallas kernels: 52.9 us -> 50.4 us
    pallas_call x1, Pallas kernels: 52.9 us -> 50.4 us  [local(): pl.pallas_call(kernel, out_shape=jax.ShapeDtypeStruct((20, 2048), bf16),...]
where the time goes in v4:
time: 52.1 us; the launch traced here: 52 us
  Pallas kernels  50.4 us (97%)
  local copies, waits for them, and re-layouts  1.54 us (3%)
    pallas_call x1, Pallas kernels, local(): pl.pallas_call(kernel, out_shape=jax.ShapeDtypeStruct((20, 2048), bf16),...  50.4 us
    unnamed x1, local copies, waits for them, and re-layouts  1.54 us

profile of v4, /device:TPU:1, one launch (start us, length us, event | category | flops | bytes accessed | tf_op | source)
XLA Modules:
  0.0 52.0 jit_solution(2732731553977086237)
XLA Ops:
  0.0 50.4 %shard_map.100 = bf16[20,2048]{1,0:T(8,128)(2,1)} custom-call(bf16[80,2,512]{2,1,0:T(2,128)(2,1)} %bitcast.19, bf16[432,512]{1,0:T(8,128)(2,1)} %bitcast.18, f32[1,16]{1,0:T(1,128)} %bitcast.23, bf16[64,4096]{1,0:T(8,128)(2,1)} %emb_hbm.1, f32[1,4096]{1,0:T(1,128)} %bitcast.20, f32[1,4096]{1,0:T(1,128)} %bitcast.21, f32[1,4096]{1,0:T(1,128)} %bitcast.22, ...), custom_call_target="tpu_custom_call" | custom-call | flops 5000000000 | bytes 6000000 | tf_op jit(solution)/shard_map/pallas_call | solution.py:477
  50.5 1.5 %copy.13 = bf16[1,1,20,2048]{3,2,1,0:T(8,128)(2,1)} copy(bf16[1,1,20,2048]{3,2,1,0:T(8,128)(2,1)} %bitcast.16) | data formatting | bytes 163840

commit v5 on v4

--- a/solution.py
+++ b/solution.py
@@ -63,9 +63,9 @@
 
 def kernel(
     x_hbm, cw_hbm, cbias_hbm, emb_hbm, ebias_hbm, shift_hbm, scale_hbm, w_hbm, qg_hbm, kg_hbm,
-    o_ref,
+    arecv,
     x_ref, cw_ref, cbias_ref, emb_ref, ebias_ref, shift_ref, scale_ref, w_ref, qg_ref, kg_ref, halo_out, halo_in, ybuf, ysend, dens, gat, res, rr, wkv, wv, bias_k, gcol,
-    kt, vt, qscr, qrows, acc, asend, arecv,
+    kt, vt, qscr, qrows, acc, asend,
     local_sem, hs_sem, hr_sem, ys_sem, yr_sem, zs_sem, zr_sem, xs_sem, xr_sem, cs_sem, cr_sem,
     as_sem, ar_sem,
 ):
@@ -354,10 +354,11 @@
             extra = jnp.where(row16 == 0, inv_hi, jnp.where(row16 == 1, 1.0, jnp.where(row16 == 2, inv - inv_hi, 0.0)))
             vt[64:80, cols] = extra.astype(bf16)
 
-    def attend(*pieces):
+    def attend(half, *pieces):
+        rows = slice(half * 160, half * 160 + 160)
         cols = slice(pieces[0] * 1280, pieces[-1] * 1280 + 1280)
-        w = jnp.exp2(jnp.dot(q, kt[:, cols], preferred_element_type=f32))
-        acc[...] += nt_dot(w.astype(bf16), vt[:, cols])
+        w = jnp.exp2(jnp.dot(q[rows], kt[:, cols], preferred_element_type=f32))
+        acc[rows] += nt_dot(w.astype(bf16), vt[:, cols])
 
     for i in (1, 7, 2, 6, 3, 5, 4):
         z_copy(i, lax.rem(z + i, 8)).start()
@@ -413,31 +414,43 @@
     qr = (raw + c_q) * inv + d_q
     qs = lax.rsqrt(jnp.sum(qr * qr, axis=1, keepdims=True) * (1.0 / 128) + EPS)
     q = (qr * qs * (qg_ref[...] * kg_ref[...] * (math.log2(math.e) / math.sqrt(128.0)))).astype(bf16)
-    attend(0, 1)
-    attend(2, 3)
-    keys(7)
-    attend(4, 5)
-    attend(6, 7)
-    u = acc[...]
-    hi, lo = hi_lo(u)
-    numer = jnp.dot(jnp.concatenate([hi, lo, hi], axis=1), wv[...], preferred_element_type=f32)
-    out = numer / u[:, 65:66]
-    pad = jnp.zeros((12, 128), f32)
-    for j in range(16):
-        asend[j] = jnp.concatenate([out[j * 20 : j * 20 + 20], pad], axis=0).astype(bf16)
-
     def a_copy(i, src, slot, j):
         return pltpu.make_async_remote_copy(
             src_ref=asend.at[src], dst_ref=arecv.at[slot], send_sem=as_sem.at[i], recv_sem=ar_sem.at[i],
             device_id=(j // 8, s, j % 8), device_id_type=pl.DeviceIdType.MESH,
         )
 
-    def send_head(i, _):
-        j = lax.rem(head + i, 16)
-        a_copy(i, j, head, j).start()
-        return 0
-
-    lax.fori_loop(1, 16, send_head, 0)
+    pad = jnp.zeros((12, 128), f32)
+
+    def finish(half):
+        u = acc[half * 160 : half * 160 + 160]
+        hi, lo = hi_lo(u)
+        numer = jnp.dot(jnp.concatenate([hi, lo, hi], axis=1), wv[...], preferred_element_type=f32)
+        out = numer / u[:, 65:66]
+        for n in range(8):
+            piece = jnp.concatenate([out[n * 20 : n * 20 + 20], pad], axis=0)
+            asend[half * 8 + n] = piece.astype(bf16)
+
+        def send_head(k, _):
+            j = half * 8 + lax.rem(f + k, 8)
+
+            @pl.when(j != head)
+            def _():
+                a_copy(lax.rem(j - head + 16, 16), j, head, j).start()
+
+            return 0
+
+        lax.fori_loop(0, 8, send_head, 0)
+
+    attend(0, 0, 1)
+    attend(0, 2, 3)
+    keys(7)
+    attend(0, 4, 5)
+    attend(0, 6, 7)
+    finish(0)
+    for first in (0, 2, 4, 6):
+        attend(1, first, first + 1)
+    finish(1)
     arecv[head] = asend[head]
 
     for a, t in halo:
@@ -457,8 +470,6 @@
         return 0
 
     lax.fori_loop(1, 16, head_arrived, 0)
-    for j in range(16):
-        o_ref[:, j * 128 : (j + 1) * 128] = arecv[j, 0:20, :]
 
     def head_sent(i, _):
         j = lax.rem(head + i, 16)
@@ -476,7 +487,7 @@
     dma = pltpu.SemaphoreType.DMA
     out = pl.pallas_call(
         kernel,
-        out_shape=jax.ShapeDtypeStruct((20, 2048), bf16),
+        out_shape=jax.ShapeDtypeStruct((16, 32, 128), bf16),
         in_specs=[hbm] * 10,
         out_specs=vmem,
         scratch_shapes=[
@@ -508,7 +519,6 @@
             pltpu.VMEM((320, 128), f32),
             pltpu.VMEM((320, 128), f32),
             pltpu.VMEM((16, 32, 128), bf16),
-            pltpu.VMEM((16, 32, 128), bf16),
             dma((10,)),
             dma((9,)),
             dma((9,)),
@@ -539,7 +549,7 @@
         q_gain.reshape(1, 128),
         k_gain.reshape(1, 128),
     )
-    return out.reshape(1, 1, 20, 2048)
+    return out[:, :20, :].transpose(1, 0, 2).reshape(1, 1, 20, 2048)
 
 
 def solution(mesh):

time: 52.1 us -> 50.7 us (0.973)
  the two profiles are of different devices: /device:TPU:1 before, /device:TPU:2 now
where the time goes in v5:
time: 50.7 us; the launch traced here: 50.5 us
  Pallas kernels  48.9 us (96%)
  local copies, waits for them, and re-layouts  1.62 us (3%)
    pallas_call x1, Pallas kernels, local(): pl.pallas_call(kernel, out_shape=jax.ShapeDtypeStruct((16, 32, 128), bf16...  48.9 us

profile of v5, /device:TPU:2, one launch (start us, length us, event | category | flops | bytes accessed | tf_op | source)
XLA Modules:
  0.0 50.5 jit_solution(826019613964549341)
XLA Ops:
  0.0 48.9 %shard_map.100 = bf16[16,32,128]{2,1,0:T(8,128)(2,1)} custom-call(bf16[80,2,512]{2,1,0:T(2,128)(2,1)} %bitcast.19, bf16[432,512]{1,0:T(8,128)(2,1)} %bitcast.18, f32[1,16]{1,0:T(1,128)} %bitcast.23, bf16[64,4096]{1,0:T(8,128)(2,1)} %emb_hbm.1, f32[1,4096]{1,0:T(1,128)} %bitcast.20, f32[1,4096]{1,0:T(1,128)} %bitcast.21, f32[1,4096]{1,0:T(1,128)} %bitcast.22, ...), custom_call_target="tpu_custom_call" | custom-call | flops 5000000000 | bytes 6000000 | tf_op jit(solution)/shard_map/pallas_call | solution.py:488
  48.9 0.9 %slice_bitcast_fusion = bf16[20,16,128]{2,0,1:T(8,128)(2,1)S(1)} fusion(bf16[16,32,128]{2,1,0:T(8,128)(2,1)} %shard_map.100), kind=kLoop, calls=%fused_computation | loop fusion | bytes 163840 | tf_op jit(solution)/shard_map/transpose | solution.py:552
  49.8 0.7 %reshape.39 = bf16[1,1,20,2048]{3,2,1,0:T(8,128)(2,1)} reshape(bf16[20,16,128]{2,1,0:T(8,128)(2,1)S(1)} %copy.13) | data formatting | bytes 163840 | tf_op jit(solution)/shard_map/reshape | solution.py:552
  (1 shorter events, 0.0 us)

commit v6 on v5

--- a/solution.py
+++ b/solution.py
@@ -431,16 +431,12 @@
             piece = jnp.concatenate([out[n * 20 : n * 20 + 20], pad], axis=0)
             asend[half * 8 + n] = piece.astype(bf16)
 
-        def send_head(k, _):
+        for k in (4, 3, 5, 2, 6, 1, 7, 0):
             j = half * 8 + lax.rem(f + k, 8)
 
             @pl.when(j != head)
             def _():
                 a_copy(lax.rem(j - head + 16, 16), j, head, j).start()
-
-            return 0
-
-        lax.fori_loop(0, 8, send_head, 0)
 
     attend(0, 0, 1)
     attend(0, 2, 3)

time: 50.7 us -> 50.1 us (0.988)
  the two profiles are of different devices: /device:TPU:2 before, /device:TPU:3 now
where the time goes in v6:
time: 50.1 us; the launch traced here: 49.9 us
  Pallas kernels  48.3 us (96%)
  local copies, waits for them, and re-layouts  1.62 us (3%)
    pallas_call x1, Pallas kernels, local(): pl.pallas_call(kernel, out_shape=jax.ShapeDtypeStruct((16, 32, 128), bf16...  48.3 us

profile of v6, /device:TPU:3, one launch (start us, length us, event | category | flops | bytes accessed | tf_op | source)
XLA Modules:
  0.0 49.9 jit_solution(2368930751965992821)
XLA Ops:
  0.0 48.3 %shard_map.100 = bf16[16,32,128]{2,1,0:T(8,128)(2,1)} custom-call(bf16[80,2,512]{2,1,0:T(2,128)(2,1)} %bitcast.19, bf16[432,512]{1,0:T(8,128)(2,1)} %bitcast.18, f32[1,16]{1,0:T(1,128)} %bitcast.23, bf16[64,4096]{1,0:T(8,128)(2,1)} %emb_hbm.1, f32[1,4096]{1,0:T(1,128)} %bitcast.20, f32[1,4096]{1,0:T(1,128)} %bitcast.21, f32[1,4096]{1,0:T(1,128)} %bitcast.22, ...), custom_call_target="tpu_custom_call" | custom-call | flops 5000000000 | bytes 6000000 | tf_op jit(solution)/shard_map/pallas_call | solution.py:484
  48.3 0.9 %slice_bitcast_fusion = bf16[20,16,128]{2,0,1:T(8,128)(2,1)S(1)} fusion(bf16[16,32,128]{2,1,0:T(8,128)(2,1)} %shard_map.100), kind=kLoop, calls=%fused_computation | loop fusion | bytes 163840 | tf_op jit(solution)/shard_map/transpose | solution.py:548
  49.2 0.7 %reshape.39 = bf16[1,1,20,2048]{3,2,1,0:T(8,128)(2,1)} reshape(bf16[20,16,128]{2,1,0:T(8,128)(2,1)S(1)} %copy.13) | data formatting | bytes 163840 | tf_op jit(solution)/shard_map/reshape | solution.py:548
  (1 shorter events, 0.0 us)

commit v7 on v6

--- a/solution.py
+++ b/solution.py
@@ -258,7 +258,7 @@
             device_id=(g, s, ff), device_id_type=pl.DeviceIdType.MESH,
         )
 
-    for i in range(1, 8):
+    for i in (4, 3, 5, 2, 6, 1, 7):
         y_copy(i).start()
 
     def y_arrived(i):

time: 50.1 us -> 50.2 us (level)
  no operation moved by 1% of the time
where the time goes in v7:
time: 50.2 us; the launch traced here: 50 us
  Pallas kernels  48.4 us (96%)
  local copies, waits for them, and re-layouts  1.62 us (3%)
    pallas_call x1, Pallas kernels, local(): pl.pallas_call(kernel, out_shape=jax.ShapeDtypeStruct((16, 32, 128), bf16...  48.4 us

profile of v7, /device:TPU:3, one launch (start us, length us, event | category | flops | bytes accessed | tf_op | source)
XLA Modules:
  0.0 50.0 jit_solution(10594163201008477907)
XLA Ops:
  0.0 48.4 %shard_map.100 = bf16[16,32,128]{2,1,0:T(8,128)(2,1)} custom-call(bf16[80,2,512]{2,1,0:T(2,128)(2,1)} %bitcast.19, bf16[432,512]{1,0:T(8,128)(2,1)} %bitcast.18, f32[1,16]{1,0:T(1,128)} %bitcast.23, bf16[64,4096]{1,0:T(8,128)(2,1)} %emb_hbm.1, f32[1,4096]{1,0:T(1,128)} %bitcast.20, f32[1,4096]{1,0:T(1,128)} %bitcast.21, f32[1,4096]{1,0:T(1,128)} %bitcast.22, ...), custom_call_target="tpu_custom_call" | custom-call | flops 5000000000 | bytes 6000000 | tf_op jit(solution)/shard_map/pallas_call | solution.py:484
  48.4 0.9 %slice_bitcast_fusion = bf16[20,16,128]{2,0,1:T(8,128)(2,1)S(1)} fusion(bf16[16,32,128]{2,1,0:T(8,128)(2,1)} %shard_map.100), kind=kLoop, calls=%fused_computation | loop fusion | bytes 163840 | tf_op jit(solution)/shard_map/transpose | solution.py:548
  49.3 0.7 %reshape.39 = bf16[1,1,20,2048]{3,2,1,0:T(8,128)(2,1)} reshape(bf16[20,16,128]{2,1,0:T(8,128)(2,1)S(1)} %copy.13) | data formatting | bytes 163840 | tf_op jit(solution)/shard_map/reshape | solution.py:548
  (1 shorter events, 0.0 us)
